TPU v7x, 128 devices: a whole 4x4x4 slice. The times are simulated.
128 devices in a mesh: row: 16 (over z, y_lo, core), col: 8 (over x, y_hi).
Axes of the slice: x: 4, y: 4 (y_hi: 2, y_lo: 2; y = y_hi * 2 + y_lo), z: 4, core: 2. Of those that a mesh axis runs over, the one named last changes fastest.
Arguments:
- query_proj: float32 [2048, 80, 128], P('col', 'row'), may hold values from -6 to 6
- key_proj: float32 [2048, 80, 128], P('col', 'row'), may hold values from -6 to 6
- value_proj: float32 [2048, 80, 128], P('col', 'row'), may hold values from -6 to 6
- out_grad: float32 [2048, 80, 128], P('col', 'row'), may hold values from -12 to 12
- pair_bias: float32 [4, 2048, 2048], P(None, 'row', 'col'), may hold values from -6 to 6
- log_sum_exp: float32 [4, 80, 2048], P(None, 'row', 'col'), as said below
- correction: float32 [4, 80, 2048], P(None, 'row', 'col'), may hold values from -12 to 12
- pad_mask: int32 [2048], replicated, may hold values from 0 to 1, as said below
Outputs:
- grad_query: float32 [2048, 80, 128], P('col', 'row')
- grad_key: float32 [2048, 80, 128], P('col', 'row')
- grad_value: float32 [2048, 80, 128], P('col', 'row')
- grad_bias: float32 [4, 2048, 2048], P(None, 'row', 'col')
Inputs may be any that keep to these rules, and one draw needn't show every extreme that they name: `pad_mask`: token 0 is always a real residue, about one token in eight is padding. `log_sum_exp`: each entry lies between log(2048) + 1 and log(2048) + 3.5.
All inputs are finite; a program needn't handle non-finite values.
Results may differ from a plain program's by a relative error of at most 0.0003.
Values sent between devices are 32-bit elements; how exact they have to be, the bound alone decides.
A program may use at most 128 MiB of HBM per device.

v0:
```python
import math

import jax
import jax.numpy as jnp
from jax import lax
from jax.sharding import PartitionSpec as P


def shifted(x, axis, by):
    length = lax.axis_size(axis)
    return lax.ppermute(x, axis, [(i, (i + by) % length) for i in range(length)])


def tile_terms(
    query_proj,
    out_grad,
    log_sum_exp,
    correction,
    bias_all,
    pad_mask,
    key_tile,
    value_tile,
    source,
    head_count,
):
    highest = lax.Precision.HIGHEST
    query_rows, columns, channels = query_proj.shape
    key_rows = key_tile.shape[0]
    head_size = channels // head_count
    inv_root = 1.0 / math.sqrt(head_size)
    query_heads = query_proj.reshape(query_rows, columns, head_count, head_size)
    grad_heads = out_grad.reshape(query_rows, columns, head_count, head_size)
    key_heads = key_tile.reshape(key_rows, columns, head_count, head_size)
    value_heads = value_tile.reshape(key_rows, columns, head_count, head_size)
    first_row = source * key_rows
    bias_block = lax.dynamic_slice_in_dim(bias_all, first_row, key_rows, 1)
    alive_keys = lax.dynamic_slice_in_dim(pad_mask, first_row, key_rows, 0) == 1
    scores = jnp.einsum("ijhd,kjhd->hjik", query_heads, key_heads, precision=highest) * inv_root
    scores = scores + jnp.transpose(bias_block, (0, 2, 1))[:, None, :, :]
    softmax_w = jnp.where(
        alive_keys[None, None, None, :],
        jnp.exp(scores - log_sum_exp[:, :, :, None]),
        jnp.float32(0.0),
    )
    prob_grad = jnp.einsum("ijhd,kjhd->hjik", grad_heads, value_heads, precision=highest)
    score_grad = softmax_w * (prob_grad - correction[:, :, :, None])
    query_part = jnp.einsum("hjik,kjhd->ijhd", score_grad, key_heads, precision=highest) * inv_root
    key_part = jnp.einsum("hjik,ijhd->kjhd", score_grad, query_heads, precision=highest) * inv_root
    value_part = jnp.einsum("hjik,ijhd->kjhd", softmax_w, grad_heads, precision=highest)
    bias_part = jnp.transpose(jnp.sum(score_grad, axis=1), (0, 2, 1))
    return (
        query_part.reshape(query_rows, columns, channels),
        key_part.reshape(key_rows, columns, channels),
        value_part.reshape(key_rows, columns, channels),
        bias_part,
    )


def body(query_proj, key_proj, value_proj, out_grad, pair_bias, log_sum_exp, correction, pad_mask):
    head_count = pair_bias.shape[0]
    col_count = lax.axis_size("col")
    own_col = lax.axis_index("col")
    key_rows = key_proj.shape[0]
    bias_all = lax.all_gather(pair_bias, "row", axis=1, tiled=True)

    def run_tile(key_tile, value_tile, source):
        return tile_terms(
            query_proj,
            out_grad,
            log_sum_exp,
            correction,
            bias_all,
            pad_mask,
            key_tile,
            value_tile,
            source,
            head_count,
        )

    query_grad, key_first, value_first, bias_first = run_tile(key_proj, value_proj, own_col)
    bias_total = jnp.zeros((head_count, pad_mask.shape[0], query_proj.shape[0]), jnp.float32)
    bias_total = lax.dynamic_update_slice_in_dim(bias_total, bias_first, own_col * key_rows, 1)

    def advance(turn, loop_state):
        key_tile, value_tile, key_accum, value_accum, query_accum, bias_accum = loop_state
        key_tile, value_tile, key_accum, value_accum = shifted(
            (key_tile, value_tile, key_accum, value_accum), "col", 1
        )
        source = (own_col - turn) % col_count
        query_part, key_part, value_part, bias_part = run_tile(key_tile, value_tile, source)
        bias_accum = lax.dynamic_update_slice_in_dim(bias_accum, bias_part, source * key_rows, 1)
        return (
            key_tile,
            value_tile,
            key_accum + key_part,
            value_accum + value_part,
            query_accum + query_part,
            bias_accum,
        )

    loop_state = lax.fori_loop(
        1,
        col_count,
        advance,
        (key_proj, value_proj, key_first, value_first, query_grad, bias_total),
    )
    query_grad = loop_state[4]
    bias_total = loop_state[5]
    grad_key, grad_value = shifted((loop_state[2], loop_state[3]), "col", 1)
    grad_bias = lax.psum_scatter(bias_total, "row", scatter_dimension=1, tiled=True)
    return (query_grad, grad_key, grad_value, grad_bias)


def solution(mesh):
    return jax.shard_map(
        body,
        mesh=mesh,
        in_specs=(
            P("col", "row", None),
            P("col", "row", None),
            P("col", "row", None),
            P("col", "row", None),
            P(None, "row", "col"),
            P(None, "row", "col"),
            P(None, "row", "col"),
            P(),
        ),
        out_specs=(
            P("col", "row", None),
            P("col", "row", None),
            P("col", "row", None),
            P(None, "row", "col"),
        ),
        check_vma=False,
    )
```

profile of v0, /device:TPU:9, one launch (start us, length us, event | category | flops | bytes accessed | tf_op | source)
XLA Modules:
  0.0 839.2 jit_solution(18110686419295969596)
XLA Ops:
  16.7 57.7 %all-gather.2.cloned.1.call-done = f32[4,2048,256]{1,2,0:T(8,128)} async-done(((f32[4,128,256]{1,2,0:T(8,128)}), f32[4,2048,256]{1,2,0:T(8,128)}) %all-gather.2.cloned.1.call-update) | async-done | bytes 8388624 | tf_op jit(solution)/shard_map/all_gather | solution.py:64
  75.7 6.7 exponential_select_fusion.1
  82.4 4.1 fusion.16
  86.5 5.6 fusion.33
  92.2 6.0 fusion.25
  98.2 4.1 fusion.22
  106.7 598.1 %while.25 = (s32[]{:T(128)}, f32[256,5,128]{0,2,1:T(8,128)}, f32[256,5,128]{0,2,1:T(8,128)}, f32[256,5,128]{0,2,1:T(8,128)}, f32[256,5,128]{0,2,1:T(8,128)}, /*i...) while((s32[]{:T(128)}, f32[256,5,128]{0,2,1:T(8,128)}, ...), condition=%wide.region_3.4_spmd, body=%wide.region_1.3_spmd.sunk | while | flops 2526314752 | bytes 63350792 | solution.py:101
  131.8 11.4 %collective-permute-done = f32[256,5,128]{0,2,1:T(8,128)S(1)} collective-permute-done((f32[256,5,128]{0,2,1:T(8,128)}, f32[256,5,128]{0,2,1:T(8,128)S(1)}, u32[]{:S(2)}, u32[]{:S(2)}) %collective-permute-start) | collective-permute-done | bytes 655392 | tf_op jit(solution)/shard_map/while/body/eval_jaxpr/ppermute | solution.py:11
  143.2 5.6 exponential_select_fusion.3
  148.8 36.5 %collective-permute-done.1 = f32[256,5,128]{0,2,1:T(8,128)S(1)} collective-permute-done((f32[256,5,128]{0,2,1:T(8,128)}, f32[256,5,128]{0,2,1:T(8,128)S(1)}, u32[]{:S(2)}, u32[]{:S(2)}) %collective-permute-start.1) | collective-permute-done | bytes 655392 | tf_op jit(solution)/shard_map/while/body/eval_jaxpr/ppermute | solution.py:11
  185.3 5.4 fusion.60
  190.7 4.9 fusion.63
  216.4 11.8 %collective-permute-done = f32[256,5,128]{0,2,1:T(8,128)S(1)} collective-permute-done((f32[256,5,128]{0,2,1:T(8,128)}, f32[256,5,128]{0,2,1:T(8,128)S(1)}, u32[]{:S(2)}, u32[]{:S(2)}) %collective-permute-start) | collective-permute-done | bytes 655392 | tf_op jit(solution)/shard_map/while/body/eval_jaxpr/ppermute | solution.py:11
  228.2 5.6 exponential_select_fusion.3
  233.7 36.5 %collective-permute-done.1 = f32[256,5,128]{0,2,1:T(8,128)S(1)} collective-permute-done((f32[256,5,128]{0,2,1:T(8,128)}, f32[256,5,128]{0,2,1:T(8,128)S(1)}, u32[]{:S(2)}, u32[]{:S(2)}) %collective-permute-start.1) | collective-permute-done | bytes 655392 | tf_op jit(solution)/shard_map/while/body/eval_jaxpr/ppermute | solution.py:11
  270.3 5.4 fusion.60
  275.7 4.9 fusion.63
  294.1 3.9 collective-permute-start.1
  300.1 12.1 %collective-permute-done = f32[256,5,128]{0,2,1:T(8,128)S(1)} collective-permute-done((f32[256,5,128]{0,2,1:T(8,128)}, f32[256,5,128]{0,2,1:T(8,128)S(1)}, u32[]{:S(2)}, u32[]{:S(2)}) %collective-permute-start) | collective-permute-done | bytes 655392 | tf_op jit(solution)/shard_map/while/body/eval_jaxpr/ppermute | solution.py:11
  312.2 5.6 exponential_select_fusion.3
  317.8 36.5 %collective-permute-done.1 = f32[256,5,128]{0,2,1:T(8,128)S(1)} collective-permute-done((f32[256,5,128]{0,2,1:T(8,128)}, f32[256,5,128]{0,2,1:T(8,128)S(1)}, u32[]{:S(2)}, u32[]{:S(2)}) %collective-permute-start.1) | collective-permute-done | bytes 655392 | tf_op jit(solution)/shard_map/while/body/eval_jaxpr/ppermute | solution.py:11
  354.3 5.4 fusion.60
  359.7 4.9 fusion.63
  382.8 12.5 %collective-permute-done = f32[256,5,128]{0,2,1:T(8,128)S(1)} collective-permute-done((f32[256,5,128]{0,2,1:T(8,128)}, f32[256,5,128]{0,2,1:T(8,128)S(1)}, u32[]{:S(2)}, u32[]{:S(2)}) %collective-permute-start) | collective-permute-done | bytes 655392 | tf_op jit(solution)/shard_map/while/body/eval_jaxpr/ppermute | solution.py:11
  395.3 5.6 exponential_select_fusion.3
  400.9 36.5 %collective-permute-done.1 = f32[256,5,128]{0,2,1:T(8,128)S(1)} collective-permute-done((f32[256,5,128]{0,2,1:T(8,128)}, f32[256,5,128]{0,2,1:T(8,128)S(1)}, u32[]{:S(2)}, u32[]{:S(2)}) %collective-permute-start.1) | collective-permute-done | bytes 655392 | tf_op jit(solution)/shard_map/while/body/eval_jaxpr/ppermute | solution.py:11
  437.4 5.4 fusion.60
  442.8 4.9 fusion.63
  450.6 3.3 fusion.62
  464.6 12.9 %collective-permute-done = f32[256,5,128]{0,2,1:T(8,128)S(1)} collective-permute-done((f32[256,5,128]{0,2,1:T(8,128)}, f32[256,5,128]{0,2,1:T(8,128)S(1)}, u32[]{:S(2)}, u32[]{:S(2)}) %collective-permute-start) | collective-permute-done | bytes 655392 | tf_op jit(solution)/shard_map/while/body/eval_jaxpr/ppermute | solution.py:11
  477.5 5.6 exponential_select_fusion.3
  483.1 36.5 %collective-permute-done.1 = f32[256,5,128]{0,2,1:T(8,128)S(1)} collective-permute-done((f32[256,5,128]{0,2,1:T(8,128)}, f32[256,5,128]{0,2,1:T(8,128)S(1)}, u32[]{:S(2)}, u32[]{:S(2)}) %collective-permute-start.1) | collective-permute-done | bytes 655392 | tf_op jit(solution)/shard_map/while/body/eval_jaxpr/ppermute | solution.py:11
  519.6 5.4 fusion.60
  525.0 4.9 fusion.63
  545.6 13.1 %collective-permute-done = f32[256,5,128]{0,2,1:T(8,128)S(1)} collective-permute-done((f32[256,5,128]{0,2,1:T(8,128)}, f32[256,5,128]{0,2,1:T(8,128)S(1)}, u32[]{:S(2)}, u32[]{:S(2)}) %collective-permute-start) | collective-permute-done | bytes 655392 | tf_op jit(solution)/shard_map/while/body/eval_jaxpr/ppermute | solution.py:11
  558.7 5.6 exponential_select_fusion.3
  564.3 36.5 %collective-permute-done.1 = f32[256,5,128]{0,2,1:T(8,128)S(1)} collective-permute-done((f32[256,5,128]{0,2,1:T(8,128)}, f32[256,5,128]{0,2,1:T(8,128)S(1)}, u32[]{:S(2)}, u32[]{:S(2)}) %collective-permute-start.1) | collective-permute-done | bytes 655392 | tf_op jit(solution)/shard_map/while/body/eval_jaxpr/ppermute | solution.py:11
  600.8 5.4 fusion.60
  606.2 4.9 fusion.63
  626.8 12.2 %collective-permute-done = f32[256,5,128]{0,2,1:T(8,128)S(1)} collective-permute-done((f32[256,5,128]{0,2,1:T(8,128)}, f32[256,5,128]{0,2,1:T(8,128)S(1)}, u32[]{:S(2)}, u32[]{:S(2)}) %collective-permute-start) | collective-permute-done | bytes 655392 | tf_op jit(solution)/shard_map/while/body/eval_jaxpr/ppermute | solution.py:11
  639.0 5.6 exponential_select_fusion.3
  644.6 36.5 %collective-permute-done.1 = f32[256,5,128]{0,2,1:T(8,128)S(1)} collective-permute-done((f32[256,5,128]{0,2,1:T(8,128)}, f32[256,5,128]{0,2,1:T(8,128)S(1)}, u32[]{:S(2)}, u32[]{:S(2)}) %collective-permute-start.1) | collective-permute-done | bytes 655392 | tf_op jit(solution)/shard_map/while/body/eval_jaxpr/ppermute | solution.py:11
  681.1 5.4 fusion.60
  686.5 4.9 fusion.63
  704.8 8.7 %copy.97 = f32[4,2048,256]{2,1,0:T(8,128)} copy(f32[4,2048,256]{1,2,0:T(8,128)} %get-tuple-element.341) | data formatting | bytes 16777216 | tf_op jit(solution)/shard_map/while | solution.py:101
  717.5 10.7 %collective-permute-done.4 = f32[256,5,128]{2,0,1:T(8,128)S(1)} collective-permute-done((f32[256,5,128]{2,0,1:T(8,128)S(1)}, f32[256,5,128]{2,0,1:T(8,128)S(1)}, u32[]{:S(2)}, u32[]{:S(2)}) %collective-permute-start.4) | collective-permute-done | bytes 655392 | tf_op jit(solution)/shard_map/ppermute | solution.py:11
  728.1 21.6 %collective-permute-done.5 = f32[256,5,128]{2,0,1:T(8,128)S(1)} collective-permute-done((f32[256,5,128]{2,0,1:T(8,128)S(1)}, f32[256,5,128]{2,0,1:T(8,128)S(1)}, u32[]{:S(2)}, u32[]{:S(2)}) %collective-permute-start.5) | collective-permute-done | bytes 655392 | tf_op jit(solution)/shard_map/ppermute | solution.py:11
  749.7 80.6 %reduce-scatter.2.cloned.1.call-done = f32[4,128,256]{2,1,0:T(8,128)} async-done(((f32[4,2048,256]{2,1,0:T(8,128)}), f32[4,128,256]{2,1,0:T(8,128)}) %reduce-scatter.2.cloned.1.call-update) | async-done | bytes 524304 | tf_op jit(solution)/shard_map/reduce_scatter | solution.py:110
  (138 shorter events, 142.0 us)
Async XLA Ops:
  7.2 8.5 %copy-start.2 = (f32[256,5,128]{2,0,1:T(8,128)S(1)}, f32[256,5,128]{2,0,1:T(8,128)}, u32[]{:S(2)}) copy-start(f32[256,5,128]{2,0,1:T(8,128)} %param.13) | copy-start | bytes 1966084
  7.2 67.2 %all-gather.2.cloned.1.call-start = ((), (), s32[]{:S(2)}) async-start(), calls=%async_computation.1 | async-start | bytes 8912896 | tf_op jit(solution)/shard_map/all_gather | solution.py:64
  9.3 820.9 %reduce-scatter.2.cloned.1.call-start = ((), (), s32[]{:S(2)}) async-start(), calls=%async_computation.2 | async-start | bytes 8912896 | tf_op jit(solution)/shard_map/reduce_scatter | solution.py:110
  15.7 70.8 %copy-start.1 = (f32[256,5,128]{0,2,1:T(8,128)}, f32[256,5,128]{0,2,1:T(8,128)S(1)}, u32[]{:S(2)}) copy-start(f32[256,5,128]{0,2,1:T(8,128)S(1)} %copy.90) | copy-start | bytes 1966084
  103.5 3.2 copy-start
  123.2 20.0 %collective-permute-start = (f32[256,5,128]{0,2,1:T(8,128)}, f32[256,5,128]{0,2,1:T(8,128)S(1)}, u32[]{:S(2)}, u32[]{:S(2)}) collective-permute-start(f32[256,5,128]{0,2,1:T(8,128)} %get-tuple-element.538), channel_id=1, source_target_pairs={{0,1},{1,2},{2,3},{3,4},{4,5},{5,6},{6,7},{7,0},{8,9},{9,10},{10,1... | collective-permute-start | bytes 1966088 | tf_op jit(solution)/shard_map/while/body/eval_jaxpr/ppermute | solution.py:11
  123.8 78.1 %collective-permute-start.3 = (f32[256,5,128]{0,2,1:T(8,128)}, f32[256,5,128]{0,2,1:T(8,128)}, u32[]{:S(2)}, u32[]{:S(2)}) collective-permute-start(f32[256,5,128]{0,2,1:T(8,128)} %get-tuple-element.541), channel_id=1, source_target_pairs={{0,1},{1,2},{2,3},{3,4},{4,5},{5,6},{6,7},{7,0},{8,9},{9,10},{10,1... | collective-permute-start | bytes 1966088 | tf_op jit(solution)/shard_map/while/body/eval_jaxpr/ppermute | solution.py:11
  125.8 81.3 %collective-permute-start.2 = (f32[256,5,128]{0,2,1:T(8,128)}, f32[256,5,128]{0,2,1:T(8,128)}, u32[]{:S(2)}, u32[]{:S(2)}) collective-permute-start(f32[256,5,128]{0,2,1:T(8,128)} %get-tuple-element.540), channel_id=1, source_target_pairs={{0,1},{1,2},{2,3},{3,4},{4,5},{5,6},{6,7},{7,0},{8,9},{9,10},{10,1... | collective-permute-start | bytes 1966088 | tf_op jit(solution)/shard_map/while/body/eval_jaxpr/ppermute | solution.py:11
  127.7 57.7 %collective-permute-start.1 = (f32[256,5,128]{0,2,1:T(8,128)}, f32[256,5,128]{0,2,1:T(8,128)S(1)}, u32[]{:S(2)}, u32[]{:S(2)}) collective-permute-start(f32[256,5,128]{0,2,1:T(8,128)} %get-tuple-element.539), channel_id=1, source_target_pairs={{0,1},{1,2},{2,3},{3,4},{4,5},{5,6},{6,7},{7,0},{8,9},{9,10},{10,1... | collective-permute-start | bytes 1966088 | tf_op jit(solution)/shard_map/while/body/eval_jaxpr/ppermute | solution.py:11
  209.2 19.0 %collective-permute-start = (f32[256,5,128]{0,2,1:T(8,128)}, f32[256,5,128]{0,2,1:T(8,128)S(1)}, u32[]{:S(2)}, u32[]{:S(2)}) collective-permute-start(f32[256,5,128]{0,2,1:T(8,128)} %get-tuple-element.538), channel_id=1, source_target_pairs={{0,1},{1,2},{2,3},{3,4},{4,5},{5,6},{6,7},{7,0},{8,9},{9,10},{10,1... | collective-permute-start | bytes 1966088 | tf_op jit(solution)/shard_map/while/body/eval_jaxpr/ppermute | solution.py:11
  209.2 77.6 %collective-permute-start.3 = (f32[256,5,128]{0,2,1:T(8,128)}, f32[256,5,128]{0,2,1:T(8,128)}, u32[]{:S(2)}, u32[]{:S(2)}) collective-permute-start(f32[256,5,128]{0,2,1:T(8,128)} %get-tuple-element.541), channel_id=1, source_target_pairs={{0,1},{1,2},{2,3},{3,4},{4,5},{5,6},{6,7},{7,0},{8,9},{9,10},{10,1... | collective-permute-start | bytes 1966088 | tf_op jit(solution)/shard_map/while/body/eval_jaxpr/ppermute | solution.py:11
  210.4 81.7 %collective-permute-start.2 = (f32[256,5,128]{0,2,1:T(8,128)}, f32[256,5,128]{0,2,1:T(8,128)}, u32[]{:S(2)}, u32[]{:S(2)}) collective-permute-start(f32[256,5,128]{0,2,1:T(8,128)} %get-tuple-element.540), channel_id=1, source_target_pairs={{0,1},{1,2},{2,3},{3,4},{4,5},{5,6},{6,7},{7,0},{8,9},{9,10},{10,1... | collective-permute-start | bytes 1966088 | tf_op jit(solution)/shard_map/while/body/eval_jaxpr/ppermute | solution.py:11
  211.4 58.9 %collective-permute-start.1 = (f32[256,5,128]{0,2,1:T(8,128)}, f32[256,5,128]{0,2,1:T(8,128)S(1)}, u32[]{:S(2)}, u32[]{:S(2)}) collective-permute-start(f32[256,5,128]{0,2,1:T(8,128)} %get-tuple-element.539), channel_id=1, source_target_pairs={{0,1},{1,2},{2,3},{3,4},{4,5},{5,6},{6,7},{7,0},{8,9},{9,10},{10,1... | collective-permute-start | bytes 1966088 | tf_op jit(solution)/shard_map/while/body/eval_jaxpr/ppermute | solution.py:11
  294.1 18.1 %collective-permute-start = (f32[256,5,128]{0,2,1:T(8,128)}, f32[256,5,128]{0,2,1:T(8,128)S(1)}, u32[]{:S(2)}, u32[]{:S(2)}) collective-permute-start(f32[256,5,128]{0,2,1:T(8,128)} %get-tuple-element.538), channel_id=1, source_target_pairs={{0,1},{1,2},{2,3},{3,4},{4,5},{5,6},{6,7},{7,0},{8,9},{9,10},{10,1... | collective-permute-start | bytes 1966088 | tf_op jit(solution)/shard_map/while/body/eval_jaxpr/ppermute | solution.py:11
  294.1 76.7 %collective-permute-start.3 = (f32[256,5,128]{0,2,1:T(8,128)}, f32[256,5,128]{0,2,1:T(8,128)}, u32[]{:S(2)}, u32[]{:S(2)}) collective-permute-start(f32[256,5,128]{0,2,1:T(8,128)} %get-tuple-element.541), channel_id=1, source_target_pairs={{0,1},{1,2},{2,3},{3,4},{4,5},{5,6},{6,7},{7,0},{8,9},{9,10},{10,1... | collective-permute-start | bytes 1966088 | tf_op jit(solution)/shard_map/while/body/eval_jaxpr/ppermute | solution.py:11
  294.1 82.0 %collective-permute-start.2 = (f32[256,5,128]{0,2,1:T(8,128)}, f32[256,5,128]{0,2,1:T(8,128)}, u32[]{:S(2)}, u32[]{:S(2)}) collective-permute-start(f32[256,5,128]{0,2,1:T(8,128)} %get-tuple-element.540), channel_id=1, source_target_pairs={{0,1},{1,2},{2,3},{3,4},{4,5},{5,6},{6,7},{7,0},{8,9},{9,10},{10,1... | collective-permute-start | bytes 1966088 | tf_op jit(solution)/shard_map/while/body/eval_jaxpr/ppermute | solution.py:11
  294.1 60.2 %collective-permute-start.1 = (f32[256,5,128]{0,2,1:T(8,128)}, f32[256,5,128]{0,2,1:T(8,128)S(1)}, u32[]{:S(2)}, u32[]{:S(2)}) collective-permute-start(f32[256,5,128]{0,2,1:T(8,128)} %get-tuple-element.539), channel_id=1, source_target_pairs={{0,1},{1,2},{2,3},{3,4},{4,5},{5,6},{6,7},{7,0},{8,9},{9,10},{10,1... | collective-permute-start | bytes 1966088 | tf_op jit(solution)/shard_map/while/body/eval_jaxpr/ppermute | solution.py:11
  378.1 17.2 %collective-permute-start = (f32[256,5,128]{0,2,1:T(8,128)}, f32[256,5,128]{0,2,1:T(8,128)S(1)}, u32[]{:S(2)}, u32[]{:S(2)}) collective-permute-start(f32[256,5,128]{0,2,1:T(8,128)} %get-tuple-element.538), channel_id=1, source_target_pairs={{0,1},{1,2},{2,3},{3,4},{4,5},{5,6},{6,7},{7,0},{8,9},{9,10},{10,1... | collective-permute-start | bytes 1966088 | tf_op jit(solution)/shard_map/while/body/eval_jaxpr/ppermute | solution.py:11
  378.1 75.8 %collective-permute-start.3 = (f32[256,5,128]{0,2,1:T(8,128)}, f32[256,5,128]{0,2,1:T(8,128)}, u32[]{:S(2)}, u32[]{:S(2)}) collective-permute-start(f32[256,5,128]{0,2,1:T(8,128)} %get-tuple-element.541), channel_id=1, source_target_pairs={{0,1},{1,2},{2,3},{3,4},{4,5},{5,6},{6,7},{7,0},{8,9},{9,10},{10,1... | collective-permute-start | bytes 1966088 | tf_op jit(solution)/shard_map/while/body/eval_jaxpr/ppermute | solution.py:11
  378.1 81.1 %collective-permute-start.2 = (f32[256,5,128]{0,2,1:T(8,128)}, f32[256,5,128]{0,2,1:T(8,128)}, u32[]{:S(2)}, u32[]{:S(2)}) collective-permute-start(f32[256,5,128]{0,2,1:T(8,128)} %get-tuple-element.540), channel_id=1, source_target_pairs={{0,1},{1,2},{2,3},{3,4},{4,5},{5,6},{6,7},{7,0},{8,9},{9,10},{10,1... | collective-permute-start | bytes 1966088 | tf_op jit(solution)/shard_map/while/body/eval_jaxpr/ppermute | solution.py:11
  378.1 59.3 %collective-permute-start.1 = (f32[256,5,128]{0,2,1:T(8,128)}, f32[256,5,128]{0,2,1:T(8,128)S(1)}, u32[]{:S(2)}, u32[]{:S(2)}) collective-permute-start(f32[256,5,128]{0,2,1:T(8,128)} %get-tuple-element.539), channel_id=1, source_target_pairs={{0,1},{1,2},{2,3},{3,4},{4,5},{5,6},{6,7},{7,0},{8,9},{9,10},{10,1... | collective-permute-start | bytes 1966088 | tf_op jit(solution)/shard_map/while/body/eval_jaxpr/ppermute | solution.py:11
  461.3 16.2 %collective-permute-start = (f32[256,5,128]{0,2,1:T(8,128)}, f32[256,5,128]{0,2,1:T(8,128)S(1)}, u32[]{:S(2)}, u32[]{:S(2)}) collective-permute-start(f32[256,5,128]{0,2,1:T(8,128)} %get-tuple-element.538), channel_id=1, source_target_pairs={{0,1},{1,2},{2,3},{3,4},{4,5},{5,6},{6,7},{7,0},{8,9},{9,10},{10,1... | collective-permute-start | bytes 1966088 | tf_op jit(solution)/shard_map/while/body/eval_jaxpr/ppermute | solution.py:11
  461.3 74.8 %collective-permute-start.3 = (f32[256,5,128]{0,2,1:T(8,128)}, f32[256,5,128]{0,2,1:T(8,128)}, u32[]{:S(2)}, u32[]{:S(2)}) collective-permute-start(f32[256,5,128]{0,2,1:T(8,128)} %get-tuple-element.541), channel_id=1, source_target_pairs={{0,1},{1,2},{2,3},{3,4},{4,5},{5,6},{6,7},{7,0},{8,9},{9,10},{10,1... | collective-permute-start | bytes 1966088 | tf_op jit(solution)/shard_map/while/body/eval_jaxpr/ppermute | solution.py:11
  461.3 80.1 %collective-permute-start.2 = (f32[256,5,128]{0,2,1:T(8,128)}, f32[256,5,128]{0,2,1:T(8,128)}, u32[]{:S(2)}, u32[]{:S(2)}) collective-permute-start(f32[256,5,128]{0,2,1:T(8,128)} %get-tuple-element.540), channel_id=1, source_target_pairs={{0,1},{1,2},{2,3},{3,4},{4,5},{5,6},{6,7},{7,0},{8,9},{9,10},{10,1... | collective-permute-start | bytes 1966088 | tf_op jit(solution)/shard_map/while/body/eval_jaxpr/ppermute | solution.py:11
  461.3 58.3 %collective-permute-start.1 = (f32[256,5,128]{0,2,1:T(8,128)}, f32[256,5,128]{0,2,1:T(8,128)S(1)}, u32[]{:S(2)}, u32[]{:S(2)}) collective-permute-start(f32[256,5,128]{0,2,1:T(8,128)} %get-tuple-element.539), channel_id=1, source_target_pairs={{0,1},{1,2},{2,3},{3,4},{4,5},{5,6},{6,7},{7,0},{8,9},{9,10},{10,1... | collective-permute-start | bytes 1966088 | tf_op jit(solution)/shard_map/while/body/eval_jaxpr/ppermute | solution.py:11
  543.4 15.3 %collective-permute-start = (f32[256,5,128]{0,2,1:T(8,128)}, f32[256,5,128]{0,2,1:T(8,128)S(1)}, u32[]{:S(2)}, u32[]{:S(2)}) collective-permute-start(f32[256,5,128]{0,2,1:T(8,128)} %get-tuple-element.538), channel_id=1, source_target_pairs={{0,1},{1,2},{2,3},{3,4},{4,5},{5,6},{6,7},{7,0},{8,9},{9,10},{10,1... | collective-permute-start | bytes 1966088 | tf_op jit(solution)/shard_map/while/body/eval_jaxpr/ppermute | solution.py:11
  543.4 73.9 %collective-permute-start.3 = (f32[256,5,128]{0,2,1:T(8,128)}, f32[256,5,128]{0,2,1:T(8,128)}, u32[]{:S(2)}, u32[]{:S(2)}) collective-permute-start(f32[256,5,128]{0,2,1:T(8,128)} %get-tuple-element.541), channel_id=1, source_target_pairs={{0,1},{1,2},{2,3},{3,4},{4,5},{5,6},{6,7},{7,0},{8,9},{9,10},{10,1... | collective-permute-start | bytes 1966088 | tf_op jit(solution)/shard_map/while/body/eval_jaxpr/ppermute | solution.py:11
  543.4 79.2 %collective-permute-start.2 = (f32[256,5,128]{0,2,1:T(8,128)}, f32[256,5,128]{0,2,1:T(8,128)}, u32[]{:S(2)}, u32[]{:S(2)}) collective-permute-start(f32[256,5,128]{0,2,1:T(8,128)} %get-tuple-element.540), channel_id=1, source_target_pairs={{0,1},{1,2},{2,3},{3,4},{4,5},{5,6},{6,7},{7,0},{8,9},{9,10},{10,1... | collective-permute-start | bytes 1966088 | tf_op jit(solution)/shard_map/while/body/eval_jaxpr/ppermute | solution.py:11
  543.4 57.4 %collective-permute-start.1 = (f32[256,5,128]{0,2,1:T(8,128)}, f32[256,5,128]{0,2,1:T(8,128)S(1)}, u32[]{:S(2)}, u32[]{:S(2)}) collective-permute-start(f32[256,5,128]{0,2,1:T(8,128)} %get-tuple-element.539), channel_id=1, source_target_pairs={{0,1},{1,2},{2,3},{3,4},{4,5},{5,6},{6,7},{7,0},{8,9},{9,10},{10,1... | collective-permute-start | bytes 1966088 | tf_op jit(solution)/shard_map/while/body/eval_jaxpr/ppermute | solution.py:11
  624.6 14.4 %collective-permute-start = (f32[256,5,128]{0,2,1:T(8,128)}, f32[256,5,128]{0,2,1:T(8,128)S(1)}, u32[]{:S(2)}, u32[]{:S(2)}) collective-permute-start(f32[256,5,128]{0,2,1:T(8,128)} %get-tuple-element.538), channel_id=1, source_target_pairs={{0,1},{1,2},{2,3},{3,4},{4,5},{5,6},{6,7},{7,0},{8,9},{9,10},{10,1... | collective-permute-start | bytes 1966088 | tf_op jit(solution)/shard_map/while/body/eval_jaxpr/ppermute | solution.py:11
  624.6 72.9 %collective-permute-start.3 = (f32[256,5,128]{0,2,1:T(8,128)}, f32[256,5,128]{0,2,1:T(8,128)}, u32[]{:S(2)}, u32[]{:S(2)}) collective-permute-start(f32[256,5,128]{0,2,1:T(8,128)} %get-tuple-element.541), channel_id=1, source_target_pairs={{0,1},{1,2},{2,3},{3,4},{4,5},{5,6},{6,7},{7,0},{8,9},{9,10},{10,1... | collective-permute-start | bytes 1966088 | tf_op jit(solution)/shard_map/while/body/eval_jaxpr/ppermute | solution.py:11
  624.6 78.2 %collective-permute-start.2 = (f32[256,5,128]{0,2,1:T(8,128)}, f32[256,5,128]{0,2,1:T(8,128)}, u32[]{:S(2)}, u32[]{:S(2)}) collective-permute-start(f32[256,5,128]{0,2,1:T(8,128)} %get-tuple-element.540), channel_id=1, source_target_pairs={{0,1},{1,2},{2,3},{3,4},{4,5},{5,6},{6,7},{7,0},{8,9},{9,10},{10,1... | collective-permute-start | bytes 1966088 | tf_op jit(solution)/shard_map/while/body/eval_jaxpr/ppermute | solution.py:11
  624.6 56.5 %collective-permute-start.1 = (f32[256,5,128]{0,2,1:T(8,128)}, f32[256,5,128]{0,2,1:T(8,128)S(1)}, u32[]{:S(2)}, u32[]{:S(2)}) collective-permute-start(f32[256,5,128]{0,2,1:T(8,128)} %get-tuple-element.539), channel_id=1, source_target_pairs={{0,1},{1,2},{2,3},{3,4},{4,5},{5,6},{6,7},{7,0},{8,9},{9,10},{10,1... | collective-permute-start | bytes 1966088 | tf_op jit(solution)/shard_map/while/body/eval_jaxpr/ppermute | solution.py:11
  714.9 13.2 %collective-permute-start.4 = (f32[256,5,128]{2,0,1:T(8,128)S(1)}, f32[256,5,128]{2,0,1:T(8,128)S(1)}, u32[]{:S(2)}, u32[]{:S(2)}) collective-permute-start(f32[256,5,128]{2,0,1:T(8,128)S(1)} %copy.95), channel_id=1, source_target_pairs={{0,1},{1,2},{2,3},{3,4},{4,5},{5,6},{6,7},{7,0},{8,9},{9,10},{10,1... | collective-permute-start | bytes 1966088 | tf_op jit(solution)/shard_map/ppermute | solution.py:11
  716.3 33.4 %collective-permute-start.5 = (f32[256,5,128]{2,0,1:T(8,128)S(1)}, f32[256,5,128]{2,0,1:T(8,128)S(1)}, u32[]{:S(2)}, u32[]{:S(2)}) collective-permute-start(f32[256,5,128]{2,0,1:T(8,128)S(1)} %copy.96), channel_id=1, source_target_pairs={{0,1},{1,2},{2,3},{3,4},{4,5},{5,6},{6,7},{7,0},{8,9},{9,10},{10,1... | collective-permute-start | bytes 1966088 | tf_op jit(solution)/shard_map/ppermute | solution.py:11
Sparse Core Ops, SparseCore 0:
  10.2 64.1 all-gather.1
  713.7 116.5 reduce-scatter.1
where the time goes:
time: 853 us; the launch traced here: 839 us
  waiting for transfers between devices  512 us (60%)
  matrix products  183 us (21%)
  local copies, waits for them, and re-layouts  57 us (7%)
  other arithmetic  35.2 us (4%)
  starting transfers between devices  19.8 us (2%)
  loops' own time  17.1 us (2%)
  between operations  14.6 us (2%)
    ppermute x30, waiting for transfers between devices, shifted(): lax.ppermute(x, axis, [(i, (i + by) % length) for i in range(length)])  374 us
    reduce_scatter x1, waiting for transfers between devices, body(): lax.psum_scatter(bias_total, 'row', scatter_dimension=1, tiled=True)  80.6 us
    all_gather x1, waiting for transfers between devices, body(): bias_all = lax.all_gather(pair_bias, 'row', axis=1, tiled=True)  57.7 us
    dot_general x8, matrix products, tile_terms(): jnp.einsum('ijhd,kjhd->hjik', query_heads, key_heads, precision=highest)  45.8 us
    dot_general x8, matrix products, tile_terms(): jnp.einsum('ijhd,kjhd->hjik', grad_heads, value_heads, precision=highest)  43.2 us
    dot_general x8, matrix products, tile_terms(): jnp.einsum('hjik,kjhd->ijhd', score_grad, key_heads, precision=highest)  40.2 us
    dot_general x8, matrix products, tile_terms(): jnp.einsum('hjik,ijhd->kjhd', softmax_w, grad_heads, precision=highest)  27 us
    dot_general x8, matrix products, tile_terms(): jnp.einsum('hjik,ijhd->kjhd', score_grad, query_heads, precision=highest)  27 us
  transfers between devices with their start and end apart: 32, of which 18 were waited for; matrix products, arithmetic and copies ran while one was open for 26% of the time, Pallas kernels for 0%

commit v1 on v0

v1 whole, which is shorter than its diff:
```python
import functools
import math

import jax
import jax.numpy as jnp
from jax import lax
from jax.experimental import pallas as pl
from jax.experimental.pallas import tpu as pltpu
from jax.sharding import PartitionSpec as P

LOG2E = math.log2(math.e)
ROOT = 1.0 / math.sqrt(32)
BF = jnp.bfloat16
F32 = jnp.float32
MESH = pl.DeviceIdType.MESH


def place(z, a, k, x, b):
    return (z * 4 + a * 2 + k, x * 2 + b)


def dg(lhs, rhs, lhs_dim, rhs_dim):
    return lax.dot_general(
        lhs, rhs, (((lhs_dim,), (rhs_dim,)), ((), ())), preferred_element_type=F32
    )


def split(x):
    hi = x.astype(BF)
    return hi, (x - hi.astype(F32)).astype(BF)


def extra_rows(x):
    hi = x.astype(BF)
    rest = x - hi.astype(F32)
    mid = rest.astype(BF)
    low = (rest - mid.astype(F32)).astype(BF)
    row = lax.broadcasted_iota(jnp.int32, (32, x.shape[1]), 0)
    out = jnp.where(
        row == 0,
        hi.astype(F32),
        jnp.where(row == 1, mid.astype(F32), jnp.where(row == 2, low.astype(F32), 0.0)),
    )
    return out.astype(BF)


def key_rows(x):
    hi, low = split(x)
    ones = jnp.ones((32, x.shape[1]), BF)
    return hi, low, jnp.concatenate([hi, low, hi, ones], axis=0)


def pack_queries(half, qgb, lrb, qp, gp):
    cols = slice(256 * half, 256 * half + 256)

    def step(t, carry):
        src = t // 5
        j = t % 5
        for h in range(2):
            rows = slice(32 * h, 32 * h + 32)
            level = lrb[half, src, 0, h, pl.ds(j, 1), :] * (-LOG2E)
            corr = -lrb[half, src, 1, h, pl.ds(j, 1), :]
            for which, packed, scale, row in ((0, qp, LOG2E * ROOT, level), (1, gp, None, corr)):
                x = qgb[half, src, which, j, rows, :]
                hi, low = split(x if scale is None else x * scale)
                packed[src, j, h, 0:32, cols] = hi
                packed[src, j, h, 32:64, cols] = hi
                packed[src, j, h, 64:96, cols] = low
                packed[src, j, h, 96:128, cols] = extra_rows(row)
        return carry

    lax.fori_loop(0, 10, step, 0)


def compute_block(kv, qp, gp, bias, dkv, dqb, db, scr, first):
    for half in range(2):
        for part in range(2):
            for h in range(2):
                db[half, part, h] = jnp.zeros((128, 256), F32)

    def step(t, carry):
        src = t // 5
        j = t % 5
        for h in range(2):
            w_hi, w_low, s_hi, s_low = [scr.at[h, i] for i in range(4)]
            rows = slice(32 * h, 32 * h + 32)
            k_hi, k_low, kp = key_rows(kv[src, 0, j, rows, :])
            _, _, vp = key_rows(kv[src, 1, j, rows, :])
            for half in range(2):
                cols = slice(256 * half, 256 * half + 256)
                st = dg(kp, qp[src, j, h, :, cols], 0, 0)
                pt = dg(vp, gp[src, j, h, :, cols], 0, 0)
                for part in range(2):
                    keys = slice(128 * part, 128 * part + 128)
                    w = jnp.exp2(st[keys] + bias[half, part, h])
                    ds = w * pt[keys]
                    db[half, part, h] += ds
                    w_hi[keys, cols], w_low[keys, cols] = split(w)
                    s_hi[keys, cols], s_low[keys, cols] = split(ds)
            k2 = jnp.concatenate([k_hi, k_low], axis=0)
            r = dg(k2, s_hi[...], 1, 0)
            total = (r[:32] + r[32:] + dg(k_hi, s_low[...], 1, 0)) * ROOT
            for half in range(2):
                mine = total[:, 256 * half : 256 * half + 256]
                dqb[half, src, j, rows, :] = jnp.where(first, mine, dqb[half, src, j, rows, :] + mine)
            r = dg(qp[src, j, h, 32:96, :], s_hi[...], 1, 1)
            r2 = dg(qp[src, j, h, 0:32, :], s_low[...], 1, 1)
            dkv[src, 0, j, rows, :] = (r[:32] + r[32:] + r2) * (1.0 / LOG2E)
            r = dg(gp[src, j, h, 32:96, :], w_hi[...], 1, 1)
            r2 = dg(gp[src, j, h, 0:32, :], w_low[...], 1, 1)
            dkv[src, 1, j, rows, :] = r[:32] + r[32:] + r2
        return carry

    lax.fori_loop(0, 10, step, 0)


def kernel(
    q_ref, k_ref, v_ref, g_ref, b_ref, l_ref, r_ref, m_ref,
    dq_ref, dk_ref, dv_ref, db_ref,
    skv, sqg, sbb, slr, kvb, qgb, lrb, bb, dkv, rkv, dqb, rdq, dbb, rb, rbb, qp, gp, scr,
    kvs, kvr, qgs, qgr, lrs, lrr, b1s, b1r, b2s, b2r, dks, dkr, dqs, dqr, dbs, dbr, d1s, d1r,
):
    row = lax.axis_index("row")
    col = lax.axis_index("col")
    z = row // 4
    a = (row // 2) % 2
    k = row % 2
    x = col // 2
    b = col % 2

    def at(dz=0, dx=0, dk=0):
        return place((z + dz) % 4, a, (k + dk) % 2, (x + dx) % 4, b)

    barrier = pltpu.get_barrier_semaphore()
    partners = [at(dx=dx, dk=dk) for dx in (1, 2, 3) for dk in (0, 1)]
    partners += [at(dz=dz) for dz in (1, 2, 3)]
    for da in (0, 1):
        for dy in (0, 1):
            for dk in (0, 1):
                if da or dy or dk:
                    partners.append(place(z, (a + da) % 2, (k + dk) % 2, x, (b + dy) % 2))
    for partner in partners:
        pl.semaphore_signal(barrier, inc=1, device_id=partner, device_id_type=MESH)

    def remote(src, dst, send, recv, target):
        return pltpu.make_async_remote_copy(
            src_ref=src, dst_ref=dst, send_sem=send, recv_sem=recv,
            device_id=target, device_id_type=MESH,
        )

    def done(ref, sem):
        pltpu.make_async_copy(ref, ref, sem).wait()

    def turn(ref, dst, which):
        for j in range(5):
            t = ref[:, j, :].T
            dst[0, which, j] = t[:64]
            dst[1, which, j] = t[64:]

    alive = jnp.broadcast_to(m_ref[pl.ds(row, 1), :], (128, 128)).astype(F32).T
    alive = jnp.concatenate([alive, alive], axis=1) == 1.0
    for h in range(4):
        sbb[h // 2, h % 2] = jnp.where(alive, b_ref[h] * LOG2E, -1e30)
    for d in range(2):
        for h in range(2):
            slr[d, 0, h] = l_ref[2 * d + h]
            slr[d, 1, h] = r_ref[2 * d + h]

    pl.semaphore_wait(barrier, len(partners))

    for da in (0, 1):
        for dk in (0, 1):
            a_to = (a + da) % 2
            d = (k + dk) % 2
            copy = remote(
                sbb.at[d], bb.at[z, b, k], b1s.at[da, dk], b1r.at[b, k], place(z, a_to, d, x, a)
            )
            if da == 0 and dk == 0:
                pl.when(a == b)(
                    lambda: pltpu.make_async_copy(sbb.at[k], bb.at[z, b, k], b1r.at[b, k]).start()
                )
                pl.when(a != b)(copy.start)
            else:
                copy.start()

    turn(k_ref, skv, 0)
    turn(v_ref, skv, 1)
    pltpu.make_async_copy(skv.at[k], kvb.at[x, k], kvr.at[x, k]).start()
    for dx, dk in ((0, 1), (1, 0), (3, 0), (1, 1), (3, 1), (2, 0), (2, 1)):
        remote(
            skv.at[(k + dk) % 2], kvb.at[x, k], kvs.at[dx, dk], kvr.at[x, k], at(dx=dx, dk=dk)
        ).start()

    turn(q_ref, sqg, 0)
    turn(g_ref, sqg, 1)
    pltpu.make_async_copy(sqg.at[k], qgb.at[b, k], qgr.at[b, k]).start()
    pltpu.make_async_copy(slr.at[k], lrb.at[b, k], lrr.at[b, k]).start()
    for dy, dk in ((0, 1), (1, 0), (1, 1)):
        d = (k + dk) % 2
        target = place(z, a, d, x, (b + dy) % 2)
        remote(slr.at[d], lrb.at[b, k], lrs.at[dy, dk], lrr.at[b, k], target).start()
        remote(sqg.at[d], qgb.at[b, k], qgs.at[dy, dk], qgr.at[b, k], target).start()

    for half in range(2):
        for part in range(2):
            done(bb.at[z, half, part], b1r.at[half, part])
    for dz in (1, 3, 2):
        remote(bb.at[z], bb.at[z], b2s.at[dz], b2r.at[z], at(dz=dz)).start()

    for half in range(2):
        for src in range(2):
            done(lrb.at[half, src], lrr.at[half, src])
            done(qgb.at[half, src], qgr.at[half, src])
        pack_queries(half, qgb, lrb, qp, gp)

    def block(t, carry):
        dx = (t + t // 2 - 2 * (t // 3)) % 4
        xk = (x + dx) % 4
        for src in range(2):
            done(kvb.at[xk, src], kvr.at[xk, src])
        pl.when(xk != z)(lambda: done(bb.at[xk], b2r.at[xk]))
        compute_block(kvb.at[xk], qp, gp, bb.at[xk], dkv.at[xk], dqb, dbb.at[xk], scr, t == 0)
        pl.when(xk != z)(
            remote(dbb.at[xk], rb.at[z], dbs.at[xk], dbr.at[z], place(xk, a, k, x, b)).start
        )
        for dk in (0, 1):
            d = (k + dk) % 2
            copy = remote(
                dkv.at[xk, d], rkv.at[x, k], dks.at[dx, dk], dkr.at[x, k], place(z, a, d, xk, b)
            )
            if dk == 0:
                pl.when(dx != 0)(copy.start)
            else:
                copy.start()
        return carry

    lax.fori_loop(0, 4, block, 0)

    for dy, dk in ((1, 0), (1, 1), (0, 1)):
        d = (k + dk) % 2
        to = (b + dy) % 2
        remote(
            dqb.at[to, d], rdq.at[b, k], dqs.at[dy, dk], dqr.at[b, k], place(z, a, d, x, to)
        ).start()

    for dz in (1, 3, 2):
        zk = (z + dz) % 4
        done(rb.at[zk], dbr.at[zk])
        for half in range(2):
            for part in range(2):
                for h in range(2):
                    dbb[z, half, part, h] += rb[zk, half, part, h]
    for dy in (0, 1):
        for dk in (0, 1):
            half = (b + dy) % 2
            part = (k + dk) % 2
            copy = remote(
                dbb.at[z, half, part], rbb.at[a, k], d1s.at[dy, dk], d1r.at[a, k],
                place(z, b, part, x, half),
            )
            if dy == 0 and dk == 0:
                pl.when(a == b)(
                    lambda: pltpu.make_async_copy(dbb.at[z, b, k], rbb.at[a, k], d1r.at[a, k]).start()
                )
                pl.when(a != b)(copy.start)
            else:
                copy.start()

    for dx in range(4):
        for dk in range(2):
            if dx or dk:
                done(rkv.at[(x + dx) % 4, (k + dk) % 2], dkr.at[(x + dx) % 4, (k + dk) % 2])
    for j in range(5):
        for which, out in ((0, dk_ref), (1, dv_ref)):
            own = dkv[x, k, which, j]
            for dx in (1, 2, 3):
                own = own + rkv[(x + dx) % 4, k, which, j]
            other = rkv[0, 1 - k, which, j]
            for xk in (1, 2, 3):
                other = other + rkv[xk, 1 - k, which, j]
            low = jnp.where(k == 0, own, other)
            high = jnp.where(k == 0, other, own)
            out[:, j, :] = jnp.concatenate([low, high], axis=0).T
    for dy, dk in ((1, 0), (1, 1), (0, 1)):
        done(rdq.at[(b + dy) % 2, (k + dk) % 2], dqr.at[(b + dy) % 2, (k + dk) % 2])
    for j in range(5):
        own = dqb[b, k, j] + rdq[1 - b, k, j]
        other = rdq[0, 1 - k, j] + rdq[1, 1 - k, j]
        low = jnp.where(k == 0, own, other)
        high = jnp.where(k == 0, other, own)
        dq_ref[:, j, :] = jnp.concatenate([low, high], axis=0).T
    for half in range(2):
        for part in range(2):
            done(rbb.at[half, part], d1r.at[half, part])
    for d in range(2):
        for h in range(2):
            db_ref[2 * d + h] = rbb[0, d, h] + rbb[1, d, h]

    for dx in range(4):
        for dk in range(2):
            if dx or dk:
                done(skv.at[0], kvs.at[dx, dk])
                done(dkv.at[0, 0], dks.at[dx, dk])
    for dy, dk in ((1, 0), (1, 1), (0, 1)):
        done(slr.at[0], lrs.at[dy, dk])
        done(sqg.at[0], qgs.at[dy, dk])
        done(dqb.at[0, 0], dqs.at[dy, dk])
    for da in (0, 1):
        for dk in (0, 1):
            if da or dk:
                done(sbb.at[0], b1s.at[da, dk])
                done(sbb.at[0], d1s.at[da, dk])

    def left():
        done(sbb.at[0], b1s.at[0, 0])
        done(sbb.at[0], d1s.at[0, 0])

    pl.when(a != b)(left)
    for dz in (1, 2, 3):
        done(bb.at[0], b2s.at[dz])
        done(dbb.at[0], dbs.at[(z + dz) % 4])


def body(query_proj, key_proj, value_proj, out_grad, pair_bias, log_sum_exp, correction, pad_mask):
    vmem = pl.BlockSpec(memory_space=pltpu.VMEM)
    f = lambda *shape: pltpu.VMEM(shape, F32)
    dma = lambda *shape: pltpu.SemaphoreType.DMA(shape)
    pair = [dma(2, 2)] * 2
    return pl.pallas_call(
        kernel,
        out_shape=[jax.ShapeDtypeStruct((256, 5, 128), F32)] * 3
        + [jax.ShapeDtypeStruct((4, 128, 256), F32)],
        in_specs=[vmem] * 8,
        out_specs=[vmem] * 4,
        scratch_shapes=[
            f(2, 2, 5, 64, 256),
            f(2, 2, 5, 64, 256),
            f(2, 2, 128, 256),
            f(2, 2, 2, 5, 256),
            f(4, 2, 2, 5, 64, 256),
            f(2, 2, 2, 5, 64, 256),
            f(2, 2, 2, 2, 5, 256),
            f(4, 2, 2, 2, 128, 256),
            f(4, 2, 2, 5, 64, 256),
            f(4, 2, 2, 5, 64, 256),
            f(2, 2, 5, 64, 256),
            f(2, 2, 5, 64, 256),
            f(4, 2, 2, 2, 128, 256),
            f(4, 2, 2, 2, 128, 256),
            f(2, 2, 2, 128, 256),
            pltpu.VMEM((2, 5, 2, 128, 512), BF),
            pltpu.VMEM((2, 5, 2, 128, 512), BF),
            pltpu.VMEM((2, 4, 256, 512), BF),
            dma(4, 2), dma(4, 2), *pair, *pair, *pair, dma(4), dma(4),
            dma(4, 2), dma(4, 2), *pair, dma(4), dma(4), *pair,
        ],
        compiler_params=pltpu.CompilerParams(
            collective_id=0, has_side_effects=True, vmem_limit_bytes=60 * 2**20
        ),
    )(
        query_proj, key_proj, value_proj, out_grad, pair_bias, log_sum_exp, correction,
        pad_mask.reshape(16, 128),
    )


def solution(mesh):
    return jax.shard_map(
        body,
        mesh=mesh,
        in_specs=(
            P("col", "row", None),
            P("col", "row", None),
            P("col", "row", None),
            P("col", "row", None),
            P(None, "row", "col"),
            P(None, "row", "col"),
            P(None, "row", "col"),
            P(),
        ),
        out_specs=(
            P("col", "row", None),
            P("col", "row", None),
            P("col", "row", None),
            P(None, "row", "col"),
        ),
        check_vma=False,
    )
```

time: 853 us -> 200 us (0.23)
  the two profiles are of different devices: /device:TPU:9 before, /device:TPU:13 now
where the time goes in v1:
time: 200 us
  Pallas kernels  184 us (92%)
  local copies, waits for them, and re-layouts  14.4 us (7%)
    pallas_call x1, Pallas kernels, body(): pl.pallas_call(kernel, out_shape=[jax.ShapeDtypeStruct((256, 5, 128), F32...  184 us
    unnamed x21, local copies, waits for them, and re-layouts  10.2 us
    pallas_call x3, local copies, waits for them, and re-layouts, body(): pl.pallas_call(kernel, out_shape=[jax.ShapeDtypeStruct((256, 5, 128), F32...  4.19 us

profile of v1, /device:TPU:13, one launch (start us, length us, event | category | flops | bytes accessed | tf_op | source)
XLA Modules:
  0.0 199.5 jit_solution(17376736163241300679)
XLA Ops:
  0.6 0.0 copy-start.6
  0.6 1.4 copy.16.l_ref
  2.0 0.0 copy-done.6
  2.0 0.6 copy.17.r_ref
  2.6 0.0 copy-start.2
  2.6 2.5 %copy.12.q_ref = f32[256,5,128]{2,1,0:T(8,128)} copy(f32[256,5,128]{2,0,1:T(8,128)} %param.8) | data formatting | bytes 1310720 | tf_op args[0]
  5.1 0.0 copy-done.2
  5.2 0.0 copy-start.3
  5.2 1.4 copy.13.k_ref
  6.6 0.0 copy-done.3
  6.6 0.0 copy-start.4
  6.6 1.4 copy.14.v_ref
  8.0 0.0 copy-done.4
  8.0 1.4 copy.15.g_ref
  9.4 184.5 %shard_map.111 = (f32[256,5,128]{2,1,0:T(8,128)}, f32[256,5,128]{2,1,0:T(8,128)}, f32[256,5,128]{2,1,0:T(8,128)}, f32[4,128,256]{2,1,0:T(8,128)}) custom-call(f32[256,5,128]{2,1,0:T(8,128)} %copy.12.q_ref, f32[256,5,128]{2,1,0:T(8,128)} %copy.13.k_ref, f32[256,5,128]{2,1,0:T(8,128)} %copy.14.v_ref, f32[256,5,128]{2,1,0:T(8,128)} %copy.15.g_ref, ...), custom_call_target="tpu_custom_call" | custom-call | tf_op jit(solution)/shard_map/pallas_call | solution.py:329
  193.9 0.0 copy-start.1
  193.9 2.3 %copy.18 = f32[256,5,128]{2,0,1:T(8,128)} copy(f32[256,5,128]{2,1,0:T(8,128)} %get-tuple-element.4) | data formatting | bytes 1310720 | tf_op jit(solution)/shard_map/pallas_call | solution.py:329
  196.2 0.0 copy-done.1
  196.2 0.0 copy-start
  196.2 1.0 copy.19
  197.1 0.5 copy-done
  197.6 0.0 copy-start.5
  197.6 1.0 copy.20
  198.6 0.1 copy-done.5
  198.7 0.8 copy.22
Async XLA Ops:
  0.6 1.4 copy-start.6
  2.6 2.5 %copy-start.2 = (f32[256,5,128]{2,0,1:T(8,128)S(1)}, f32[256,5,128]{2,0,1:T(8,128)}, u32[]{:S(2)}) copy-start(f32[256,5,128]{2,0,1:T(8,128)} %param.9) | copy-start | bytes 1966084
  5.2 1.4 copy-start.3
  6.6 1.4 copy-start.4
  193.9 2.3 %copy-start.1 = (f32[256,5,128]{2,1,0:T(8,128)S(1)}, f32[256,5,128]{2,1,0:T(8,128)}, u32[]{:S(2)}) copy-start(f32[256,5,128]{2,1,0:T(8,128)} %get-tuple-element.5) | copy-start | bytes 1966084
  196.2 1.5 copy-start
  197.6 1.1 copy-start.5

commit v2 on v1

v2 whole, which is shorter than its diff:
```python
import functools
import math

import jax
import jax.numpy as jnp
from jax import lax
from jax.experimental import pallas as pl
from jax.experimental.pallas import tpu as pltpu
from jax.sharding import PartitionSpec as P

LOG2E = math.log2(math.e)
ROOT = 1.0 / math.sqrt(32)
BF = jnp.bfloat16
F32 = jnp.float32
MESH = pl.DeviceIdType.MESH


def place(z, a, k, x, b):
    return (z * 4 + a * 2 + k, x * 2 + b)


def dg(lhs, rhs, lhs_dim, rhs_dim):
    return lax.dot_general(
        lhs, rhs, (((lhs_dim,), (rhs_dim,)), ((), ())), preferred_element_type=F32
    )


def split(x):
    hi = x.astype(BF)
    return hi, (x - hi.astype(F32)).astype(BF)


def extra_rows(x):
    hi = x.astype(BF)
    rest = x - hi.astype(F32)
    mid = rest.astype(BF)
    low = (rest - mid.astype(F32)).astype(BF)
    row = lax.broadcasted_iota(jnp.int32, (32, x.shape[1]), 0)
    out = jnp.where(
        row == 0,
        hi.astype(F32),
        jnp.where(row == 1, mid.astype(F32), jnp.where(row == 2, low.astype(F32), 0.0)),
    )
    return out.astype(BF)


def key_rows(x):
    hi, low = split(x)
    ones = jnp.ones((32, x.shape[1]), BF)
    return hi, low, jnp.concatenate([hi, low, hi, ones], axis=0)


def pack_queries(h, qgb, lrb, qp, gp):
    def step(j, carry):
        for src in range(2):
            for half in range(2):
                cols = slice(256 * half, 256 * half + 256)
                level = lrb[half, src, 0, h, pl.ds(j, 1), :] * (-LOG2E)
                corr = -lrb[half, src, 1, h, pl.ds(j, 1), :]
                for which, packed, scale, row in (
                    (0, qp, LOG2E * ROOT, level),
                    (1, gp, None, corr),
                ):
                    x = qgb[h, half, src, which, j]
                    hi, low = split(x if scale is None else x * scale)
                    packed[h, src, j, 0:32, cols] = hi
                    packed[h, src, j, 32:64, cols] = hi
                    packed[h, src, j, 64:96, cols] = low
                    packed[h, src, j, 96:128, cols] = extra_rows(row)
        return carry

    lax.fori_loop(0, 5, step, 0)


def compute_block(kv, qp, gp, bias, dkv, dqb, db, scr, first):
    for half in range(2):
        for part in range(2):
            db[half, part] = jnp.zeros((128, 256), F32)

    def step(j, carry):
        for src in range(2):
            w_hi, w_low, s_hi, s_low = [scr.at[src, i] for i in range(4)]
            k_hi, k_low, kp = key_rows(kv[src, 0, j])
            _, _, vp = key_rows(kv[src, 1, j])
            for half in range(2):
                cols = slice(256 * half, 256 * half + 256)
                st = dg(kp, qp[src, j, :, cols], 0, 0)
                pt = dg(vp, gp[src, j, :, cols], 0, 0)
                for part in range(2):
                    keys = slice(128 * part, 128 * part + 128)
                    w = jnp.exp2(st[keys] + bias[half, part])
                    ds = w * pt[keys]
                    db[half, part] += ds
                    w_hi[keys, cols], w_low[keys, cols] = split(w)
                    s_hi[keys, cols], s_low[keys, cols] = split(ds)
            k2 = jnp.concatenate([k_hi, k_low], axis=0)
            r = dg(k2, s_hi[...], 1, 0)
            total = (r[:32] + r[32:] + dg(k_hi, s_low[...], 1, 0)) * ROOT
            for half in range(2):
                mine = total[:, 256 * half : 256 * half + 256]
                dqb[half, src, j] = jnp.where(first, mine, dqb[half, src, j] + mine)
            r = dg(qp[src, j, 32:96, :], s_hi[...], 1, 1)
            r2 = dg(qp[src, j, 0:32, :], s_low[...], 1, 1)
            dkv[src, 0, j] = (r[:32] + r[32:] + r2) * (1.0 / LOG2E)
            r = dg(gp[src, j, 32:96, :], w_hi[...], 1, 1)
            r2 = dg(gp[src, j, 0:32, :], w_low[...], 1, 1)
            dkv[src, 1, j] = r[:32] + r[32:] + r2
        return carry

    lax.fori_loop(0, 5, step, 0)


def kernel(
    q_ref, k_ref, v_ref, g_ref, b_ref, l_ref, r_ref, m_ref,
    dq_ref, dk_ref, dv_ref, db_ref,
    skv, sqg, sbb, slr, kvb, qgb, lrb, bb, dkv, rkv, dqb, rdq, dbb, rb, rbb, qp, gp, scr,
    kvs, kvr, qgs, qgr, lrs, lrr, b1s, b1r, b2s, b2r, dks, dkr, dqs, dqr, dbs, dbr, d1s, d1r,
):
    row = lax.axis_index("row")
    col = lax.axis_index("col")
    z = row // 4
    a = (row // 2) % 2
    k = row % 2
    x = col // 2
    b = col % 2
    right, left = (x + 1) % 4, (x + 3) % 4
    up, down = (z + 1) % 4, (z + 3) % 4

    def at(dz=0, dx=0, dk=0):
        return place((z + dz) % 4, a, (k + dk) % 2, (x + dx) % 4, b)

    barrier = pltpu.get_barrier_semaphore()
    partners = [at(dx=dx, dk=dk) for dx in (1, 2, 3) for dk in (0, 1)]
    partners += [at(dz=dz) for dz in (1, 2, 3)]
    for da in (0, 1):
        for dy in (0, 1):
            for dk in (0, 1):
                if da or dy or dk:
                    partners.append(place(z, (a + da) % 2, (k + dk) % 2, x, (b + dy) % 2))
    for partner in partners:
        pl.semaphore_signal(barrier, inc=1, device_id=partner, device_id_type=MESH)

    def remote(src, dst, send, recv, target):
        return pltpu.make_async_remote_copy(
            src_ref=src, dst_ref=dst, send_sem=send, recv_sem=recv,
            device_id=target, device_id_type=MESH,
        )

    def done(ref, sem):
        pltpu.make_async_copy(ref, ref, sem).wait()

    def turn(ref, dst, which):
        for j in range(5):
            t = ref[j].T
            for d in range(2):
                for h in range(2):
                    first = 64 * d + 32 * h
                    dst[h, d, which, j] = t[first : first + 32]

    def send_bias(h):
        for da in (0, 1):
            for dk in (0, 1):
                a_to = (a + da) % 2
                d = (k + dk) % 2
                copy = remote(
                    sbb.at[h, d], bb.at[h, z, b, k], b1s.at[h, da, dk], b1r.at[h, b, k],
                    place(z, a_to, d, x, a),
                )
                if da == 0 and dk == 0:
                    own = pltpu.make_async_copy(sbb.at[h, k], bb.at[h, z, b, k], b1r.at[h, b, k])
                    pl.when(a == b)(own.start)
                    pl.when(a != b)(copy.start)
                else:
                    copy.start()

    def spread_bias(h):
        for half in range(2):
            for part in range(2):
                done(bb.at[h, z, half, part], b1r.at[h, half, part])
        for i, (to, half) in enumerate(((1, 0), (3, 1), (1, 1), (3, 0))):
            remote(
                bb.at[h, z, half], bb.at[h, z, half], b2s.at[h, i], b2r.at[h, z, half], at(dz=to)
            ).start()

    def pass_bias(h):
        done(bb.at[h, down, 0], b2r.at[h, down, 0])
        remote(
            bb.at[h, down, 0], bb.at[h, down, 0], b2s.at[h, 4], b2r.at[h, down, 0], at(dz=1)
        ).start()
        done(bb.at[h, up, 1], b2r.at[h, up, 1])
        remote(
            bb.at[h, up, 1], bb.at[h, up, 1], b2s.at[h, 5], b2r.at[h, up, 1], at(dz=3)
        ).start()

    def wait_bias(h, zk):
        def rest(half):
            passed = (half == 0) & (zk == down) | (half == 1) & (zk == up)
            pl.when((zk != z) & jnp.logical_not(passed))(
                lambda: done(bb.at[h, zk, half], b2r.at[h, zk, half])
            )

        rest(0)
        rest(1)

    def send_keys(h):
        pltpu.make_async_copy(skv.at[h, k], kvb.at[h, x, k], kvr.at[h, x, k]).start()
        for i, (dx, dk) in enumerate(((1, 0), (3, 0), (1, 1), (3, 1), (0, 1))):
            remote(
                skv.at[h, (k + dk) % 2], kvb.at[h, x, k], kvs.at[h, i], kvr.at[h, x, k],
                at(dx=dx, dk=dk),
            ).start()

    def pass_keys(h):
        done(kvb.at[h, left, 0], kvr.at[h, left, 0])
        remote(
            kvb.at[h, left, 0], kvb.at[h, left, 0], kvs.at[h, 5], kvr.at[h, left, 0], at(dx=1)
        ).start()
        done(kvb.at[h, right, 1], kvr.at[h, right, 1])
        remote(
            kvb.at[h, right, 1], kvb.at[h, right, 1], kvs.at[h, 6], kvr.at[h, right, 1], at(dx=3)
        ).start()

    def wait_keys(h, xk):
        pl.when(xk != left)(lambda: done(kvb.at[h, xk, 0], kvr.at[h, xk, 0]))
        pl.when(xk != right)(lambda: done(kvb.at[h, xk, 1], kvr.at[h, xk, 1]))

    def send_queries(h):
        pltpu.make_async_copy(sqg.at[h, k], qgb.at[h, b, k], qgr.at[h, b, k]).start()
        for dy, dk in ((1, 0), (1, 1), (0, 1)):
            d = (k + dk) % 2
            remote(
                sqg.at[h, d], qgb.at[h, b, k], qgs.at[h, dy, dk], qgr.at[h, b, k],
                place(z, a, d, x, (b + dy) % 2),
            ).start()

    def wait_queries(h):
        for half in range(2):
            for src in range(2):
                done(qgb.at[h, half, src], qgr.at[h, half, src])

    def sum_bias(h):
        for dz in (1, 3, 2):
            zk = (z + dz) % 4
            done(rb.at[h, zk], dbr.at[h, zk])
        for half in range(2):
            for part in range(2):
                dbb[h, z, half, part] += (
                    rb[h, up, half, part] + rb[h, down, half, part]
                ) + rb[h, (z + 2) % 4, half, part]
        for dy in (1, 0):
            for dk in (0, 1):
                half = (b + dy) % 2
                part = (k + dk) % 2
                copy = remote(
                    dbb.at[h, z, half, part], rbb.at[h, a, k], d1s.at[h, dy, dk], d1r.at[h, a, k],
                    place(z, b, part, x, half),
                )
                if dy == 0 and dk == 0:
                    own = pltpu.make_async_copy(dbb.at[h, z, b, k], rbb.at[h, a, k], d1r.at[h, a, k])
                    pl.when(a == b)(own.start)
                    pl.when(a != b)(copy.start)
                else:
                    copy.start()

    def send_query_grads(h):
        for dy, dk in ((1, 0), (1, 1), (0, 1)):
            d = (k + dk) % 2
            to = (b + dy) % 2
            remote(
                dqb.at[h, to, d], rdq.at[h, b, k], dqs.at[h, dy, dk], dqr.at[h, b, k],
                place(z, a, d, x, to),
            ).start()

    alive = jnp.broadcast_to(m_ref[pl.ds(row, 1), :], (128, 128)).astype(F32).T
    alive = jnp.concatenate([alive, alive], axis=1) == 1.0
    for h in range(4):
        sbb[h % 2, h // 2] = jnp.where(alive, b_ref[h] * LOG2E, -1e30)
    for d in range(2):
        for h in range(2):
            slr[d, 0, h] = l_ref[:, 2 * d + h, :]
            slr[d, 1, h] = r_ref[:, 2 * d + h, :]

    pl.semaphore_wait(barrier, len(partners))

    send_bias(0)
    turn(k_ref, skv, 0)
    turn(v_ref, skv, 1)
    send_keys(0)
    pltpu.make_async_copy(slr.at[k], lrb.at[b, k], lrr.at[b, k]).start()
    for dy, dk in ((1, 0), (1, 1), (0, 1)):
        d = (k + dk) % 2
        remote(
            slr.at[d], lrb.at[b, k], lrs.at[dy, dk], lrr.at[b, k], place(z, a, d, x, (b + dy) % 2)
        ).start()
    turn(q_ref, sqg, 0)
    turn(g_ref, sqg, 1)
    send_queries(0)
    spread_bias(0)
    pass_keys(0)
    send_keys(1)
    for half in range(2):
        for src in range(2):
            done(lrb.at[half, src], lrr.at[half, src])
    wait_queries(0)
    send_bias(1)
    send_queries(1)
    pack_queries(0, qgb, lrb, qp, gp)
    pass_bias(0)

    def block(n, carry):
        h = n // 4
        t = n % 4
        xk = (x + z + 1 + t) % 4

        @pl.when(n == 4)
        def _():
            wait_queries(1)
            pack_queries(1, qgb, lrb, qp, gp)

        wait_keys(h, xk)
        wait_bias(h, xk)
        compute_block(
            kvb.at[h, xk], qp.at[h], gp.at[h], bb.at[h, xk], dkv.at[h, xk], dqb.at[h],
            dbb.at[h, xk], scr, t == 0,
        )
        pl.when(xk != z)(
            remote(
                dbb.at[h, xk], rb.at[h, z], dbs.at[h, xk], dbr.at[h, z], place(xk, a, k, x, b)
            ).start
        )
        for dk in (0, 1):
            d = (k + dk) % 2
            copy = remote(
                dkv.at[h, xk, d], rkv.at[h, x, k], dks.at[h, xk, dk], dkr.at[h, x, k],
                place(z, a, d, xk, b),
            )
            if dk == 0:
                pl.when(xk != x)(copy.start)
            else:
                copy.start()

        @pl.when(n == 0)
        def _():
            spread_bias(1)

        @pl.when(n == 1)
        def _():
            pass_keys(1)

        @pl.when(n == 2)
        def _():
            pass_bias(1)

        @pl.when(n == 3)
        def _():
            send_query_grads(0)

        @pl.when(n == 5)
        def _():
            sum_bias(0)

        return carry

    lax.fori_loop(0, 8, block, 0)
    send_query_grads(1)
    sum_bias(1)

    for h in range(2):
        for dx in range(4):
            for dk in range(2):
                if dx or dk:
                    xk = (x + dx) % 4
                    c = (k + dk) % 2
                    done(rkv.at[h, xk, c], dkr.at[h, xk, c])

    def join(own, other):
        low = jnp.where(k == 0, own, other)
        high = jnp.where(k == 0, other, own)
        return jnp.concatenate([low, high], axis=0).T

    def rows(ref, *index):
        return jnp.concatenate([ref[(0, *index)], ref[(1, *index)]], axis=0)

    for j in range(5):
        for which, out in ((0, dk_ref), (1, dv_ref)):
            own = rows(dkv, x, k, which, j)
            for dx in (1, 2, 3):
                own = own + rows(rkv, (x + dx) % 4, k, which, j)
            other = rows(rkv, 0, 1 - k, which, j)
            for xk in (1, 2, 3):
                other = other + rows(rkv, xk, 1 - k, which, j)
            out[j] = join(own, other)
    for h in range(2):
        for dy, dk in ((1, 0), (1, 1), (0, 1)):
            done(rdq.at[h, (b + dy) % 2, (k + dk) % 2], dqr.at[h, (b + dy) % 2, (k + dk) % 2])
    for j in range(5):
        own = rows(dqb, b, k, j) + rows(rdq, 1 - b, k, j)
        other = rows(rdq, 0, 1 - k, j) + rows(rdq, 1, 1 - k, j)
        dq_ref[j] = join(own, other)
    for h in range(2):
        for half in range(2):
            for part in range(2):
                done(rbb.at[h, half, part], d1r.at[h, half, part])
        for d in range(2):
            db_ref[2 * d + h] = rbb[h, 0, d] + rbb[h, 1, d]

    for h in range(2):
        for i in range(7):
            done(skv.at[0, 0], kvs.at[h, i])
        for dx in range(4):
            done(dkv.at[0, 0, 0], dks.at[h, (x + dx) % 4, 1])
            if dx:
                done(dkv.at[0, 0, 0], dks.at[h, (x + dx) % 4, 0])
        for dy, dk in ((1, 0), (1, 1), (0, 1)):
            done(sqg.at[0, 0], qgs.at[h, dy, dk])
            done(dqb.at[0, 0, 0], dqs.at[h, dy, dk])
            done(sbb.at[0, 0], b1s.at[h, dy, dk])
            done(sbb.at[0, 0], d1s.at[h, dy, dk])
        for i in range(6):
            done(bb.at[0, 0, 0], b2s.at[h, i])
        for dz in (1, 2, 3):
            done(dbb.at[0, 0], dbs.at[h, (z + dz) % 4])
    for dy, dk in ((1, 0), (1, 1), (0, 1)):
        done(slr.at[0], lrs.at[dy, dk])

    @pl.when(a != b)
    def _():
        for h in range(2):
            done(sbb.at[0, 0], b1s.at[h, 0, 0])
            done(sbb.at[0, 0], d1s.at[h, 0, 0])


def body(query_proj, key_proj, value_proj, out_grad, pair_bias, log_sum_exp, correction, pad_mask):
    vmem = pl.BlockSpec(memory_space=pltpu.VMEM)
    f = lambda *shape: pltpu.VMEM(shape, F32)
    dma = lambda *shape: pltpu.SemaphoreType.DMA(shape)
    swap = lambda y: jnp.transpose(y, (1, 0, 2))
    pair = [dma(2, 2, 2)] * 2
    dq, dk, dv, db = pl.pallas_call(
        kernel,
        out_shape=[jax.ShapeDtypeStruct((5, 256, 128), F32)] * 3
        + [jax.ShapeDtypeStruct((4, 128, 256), F32)],
        in_specs=[vmem] * 8,
        out_specs=[vmem] * 4,
        scratch_shapes=[
            f(2, 2, 2, 5, 32, 256),
            f(2, 2, 2, 5, 32, 256),
            f(2, 2, 128, 256),
            f(2, 2, 2, 5, 256),
            f(2, 4, 2, 2, 5, 32, 256),
            f(2, 2, 2, 2, 5, 32, 256),
            f(2, 2, 2, 2, 5, 256),
            f(2, 4, 2, 2, 128, 256),
            f(2, 4, 2, 2, 5, 32, 256),
            f(2, 4, 2, 2, 5, 32, 256),
            f(2, 2, 2, 5, 32, 256),
            f(2, 2, 2, 5, 32, 256),
            f(2, 4, 2, 2, 128, 256),
            f(2, 4, 2, 2, 128, 256),
            f(2, 2, 2, 128, 256),
            pltpu.VMEM((2, 2, 5, 128, 512), BF),
            pltpu.VMEM((2, 2, 5, 128, 512), BF),
            pltpu.VMEM((2, 4, 256, 512), BF),
            dma(2, 7), dma(2, 4, 2), *pair, dma(2, 2), dma(2, 2), *pair, dma(2, 6), dma(2, 4, 2),
            dma(2, 4, 2), dma(2, 4, 2), *pair, dma(2, 4), dma(2, 4), *pair,
        ],
        compiler_params=pltpu.CompilerParams(
            collective_id=0, has_side_effects=True, vmem_limit_bytes=60 * 2**20
        ),
    )(
        swap(query_proj), swap(key_proj), swap(value_proj), swap(out_grad), pair_bias,
        swap(log_sum_exp), swap(correction), pad_mask.reshape(16, 128),
    )
    return swap(dq), swap(dk), swap(dv), db


def solution(mesh):
    return jax.shard_map(
        body,
        mesh=mesh,
        in_specs=(
            P("col", "row", None),
            P("col", "row", None),
            P("col", "row", None),
            P("col", "row", None),
            P(None, "row", "col"),
            P(None, "row", "col"),
            P(None, "row", "col"),
            P(),
        ),
        out_specs=(
            P("col", "row", None),
            P("col", "row", None),
            P("col", "row", None),
            P(None, "row", "col"),
        ),
        check_vma=False,
    )
```

time: 200 us -> 152 us (0.76)
  the two profiles are of different devices: /device:TPU:13 before, /device:TPU:11 now
where the time goes in v2:
time: 152 us
  Pallas kernels  146 us (96%)
  local copies, waits for them, and re-layouts  5.43 us (4%)
    pallas_call x1, Pallas kernels, body(): pl.pallas_call(kernel, out_shape=[jax.ShapeDtypeStruct((5, 256, 128), F32...  146 us
    unnamed x10, local copies, waits for them, and re-layouts  5.43 us

profile of v2, /device:TPU:11, one launch (start us, length us, event | category | flops | bytes accessed | tf_op | source)
XLA Modules:
  0.0 152.2 jit_solution(834906059589491288)
XLA Ops:
  0.6 146.1 %shard_map.111 = (f32[5,256,128]{2,1,0:T(8,128)}, f32[5,256,128]{2,1,0:T(8,128)}, f32[5,256,128]{2,1,0:T(8,128)}, f32[4,128,256]{2,1,0:T(8,128)}) custom-call(f32[5,256,128]{2,1,0:T(8,128)} %bitcast.13, f32[5,256,128]{2,1,0:T(8,128)} %bitcast.14, f32[5,256,128]{2,1,0:T(8,128)} %bitcast.15, f32[5,256,128]{2,1,0:T(8,128)} %bitcast.16, f32[4,128,256]{2,1,0:T(8,128)} %b_ref.1, ...), custom_call_target="tpu_custom_call" | custom-call | tf_op jit(solution)/shard_map/pallas_call | solution.py:439
  146.7 0.0 copy-start.1
  146.7 2.0 %copy.16 = f32[256,5,128]{2,0,1:T(8,128)} copy(f32[256,5,128]{2,0,1:T(8,128)} %bitcast.12) | data formatting | bytes 1310720
  148.8 0.0 copy-done.1
  148.8 0.0 copy-start
  148.8 0.8 copy.17
  149.6 0.5 copy-done
  150.1 0.0 copy-start.2
  150.1 0.8 copy.18
  150.9 0.4 copy-done.2
  151.4 0.8 copy.19
Async XLA Ops:
  146.7 2.0 %copy-start.1 = (f32[5,256,128]{2,1,0:T(8,128)S(1)}, f32[5,256,128]{2,1,0:T(8,128)}, u32[]{:S(2)}) copy-start(f32[5,256,128]{2,1,0:T(8,128)} %get-tuple-element.9) | copy-start | bytes 1966084
  148.8 1.3 copy-start
  150.1 1.3 copy-start.2

commit v3 on v2

--- a/solution.py
+++ b/solution.py
@@ -78,23 +78,30 @@
             db[half, part] = jnp.zeros((128, 256), F32)
 
     def step(j, carry):
+        keys = [None, None]
+        scores = [None, None]
+        grads = [None, None]
+        for src in range(2):
+            k_hi, k_low, kp = key_rows(kv[src, 0, j])
+            _, _, vp = key_rows(kv[src, 1, j])
+            keys[src] = (k_hi, k_low)
+            scores[src] = dg(kp, qp[src, j], 0, 0)
+            grads[src] = dg(vp, gp[src, j], 0, 0)
         for src in range(2):
             w_hi, w_low, s_hi, s_low = [scr.at[src, i] for i in range(4)]
-            k_hi, k_low, kp = key_rows(kv[src, 0, j])
-            _, _, vp = key_rows(kv[src, 1, j])
             for half in range(2):
                 cols = slice(256 * half, 256 * half + 256)
-                st = dg(kp, qp[src, j, :, cols], 0, 0)
-                pt = dg(vp, gp[src, j, :, cols], 0, 0)
                 for part in range(2):
-                    keys = slice(128 * part, 128 * part + 128)
-                    w = jnp.exp2(st[keys] + bias[half, part])
-                    ds = w * pt[keys]
+                    rows = slice(128 * part, 128 * part + 128)
+                    w = jnp.exp2(scores[src][rows, cols] + bias[half, part])
+                    ds = w * grads[src][rows, cols]
                     db[half, part] += ds
-                    w_hi[keys, cols], w_low[keys, cols] = split(w)
-                    s_hi[keys, cols], s_low[keys, cols] = split(ds)
-            k2 = jnp.concatenate([k_hi, k_low], axis=0)
-            r = dg(k2, s_hi[...], 1, 0)
+                    w_hi[rows, cols], w_low[rows, cols] = split(w)
+                    s_hi[rows, cols], s_low[rows, cols] = split(ds)
+        for src in range(2):
+            w_hi, w_low, s_hi, s_low = [scr.at[src, i] for i in range(4)]
+            k_hi, k_low = keys[src]
+            r = dg(jnp.concatenate([k_hi, k_low], axis=0), s_hi[...], 1, 0)
             total = (r[:32] + r[32:] + dg(k_hi, s_low[...], 1, 0)) * ROOT
             for half in range(2):
                 mine = total[:, 256 * half : 256 * half + 256]
@@ -113,8 +120,8 @@
 def kernel(
     q_ref, k_ref, v_ref, g_ref, b_ref, l_ref, r_ref, m_ref,
     dq_ref, dk_ref, dv_ref, db_ref,
-    skv, sqg, sbb, slr, kvb, qgb, lrb, bb, dkv, rkv, dqb, rdq, dbb, rb, rbb, qp, gp, scr,
-    kvs, kvr, qgs, qgr, lrs, lrr, b1s, b1r, b2s, b2r, dks, dkr, dqs, dqr, dbs, dbr, d1s, d1r,
+    skv, sqg, sbb, slr, kvb, qgb, lrb, bb, dkv, rkv, rel, zrel, dqb, rdq, dbb, rb, rbb, qp, gp, scr,
+    kvs, kvr, qgs, qgr, lrs, lrr, b1s, b1r, b2s, b2r, dks, dkr, rls, rlr, dqs, dqr, zls, zlr, dbs, dbr, d1s, d1r,
 ):
     row = lax.axis_index("row")
     col = lax.axis_index("col")
@@ -130,8 +137,8 @@
         return place((z + dz) % 4, a, (k + dk) % 2, (x + dx) % 4, b)
 
     barrier = pltpu.get_barrier_semaphore()
-    partners = [at(dx=dx, dk=dk) for dx in (1, 2, 3) for dk in (0, 1)]
-    partners += [at(dz=dz) for dz in (1, 2, 3)]
+    partners = [at(dx=dx, dk=dk) for dx in (1, 3) for dk in (0, 1)]
+    partners += [at(dz=dz) for dz in (1, 3)]
     for da in (0, 1):
         for dy in (0, 1):
             for dk in (0, 1):
@@ -238,15 +245,43 @@
             for src in range(2):
                 done(qgb.at[h, half, src], qgr.at[h, half, src])
 
+    def push_bias_grad(h, to, half):
+        zk = (up, down)[to]
+        remote(
+            dbb.at[h, zk, half], rb.at[h, to, half], dbs.at[h, to, half], dbr.at[h, to, half],
+            place(zk, a, k, x, b),
+        ).start()
+
+    def send_bias_grad(h, zk):
+        @pl.when(zk == (z + 2) % 4)
+        def _():
+            for half, dz in ((0, 1), (1, 3)):
+                remote(
+                    dbb.at[h, zk, half], zrel.at[h, half], zls.at[h, half], zlr.at[h, half],
+                    at(dz=dz),
+                ).start()
+
+        pl.when(zk == up)(lambda: push_bias_grad(h, 0, 1))
+        pl.when(zk == down)(lambda: push_bias_grad(h, 1, 0))
+
+    def finish_bias_grad(h, zk):
+        def finish(to):
+            half = to
+            done(zrel.at[h, half], zlr.at[h, half])
+            for part in range(2):
+                dbb[h, zk, half, part] += zrel[h, half, part]
+            push_bias_grad(h, to, half)
+
+        pl.when(zk == up)(lambda: finish(0))
+        pl.when(zk == down)(lambda: finish(1))
+
     def sum_bias(h):
-        for dz in (1, 3, 2):
-            zk = (z + dz) % 4
-            done(rb.at[h, zk], dbr.at[h, zk])
+        for to in range(2):
+            for half in range(2):
+                done(rb.at[h, to, half], dbr.at[h, to, half])
         for half in range(2):
             for part in range(2):
-                dbb[h, z, half, part] += (
-                    rb[h, up, half, part] + rb[h, down, half, part]
-                ) + rb[h, (z + 2) % 4, half, part]
+                dbb[h, z, half, part] += rb[h, 0, half, part] + rb[h, 1, half, part]
         for dy in (1, 0):
             for dk in (0, 1):
                 half = (b + dy) % 2
@@ -262,6 +297,18 @@
                 else:
                     copy.start()
 
+    def send_key_grads(h, xk, d):
+        remote(
+            dkv.at[h, xk, d], rkv.at[h, x, k], dks.at[h, xk, d], dkr.at[h, x, k],
+            place(z, a, d, xk, b),
+        ).start()
+
+    def add_passed(h, xk, d):
+        done(rel.at[h, d], rlr.at[h, d])
+        for which in range(2):
+            for j in range(5):
+                dkv[h, xk, d, which, j] += rel[h, d, which, j]
+
     def send_query_grads(h):
         for dy, dk in ((1, 0), (1, 1), (0, 1)):
             d = (k + dk) % 2
@@ -303,14 +350,16 @@
             done(lrb.at[half, src], lrr.at[half, src])
     wait_queries(0)
     send_bias(1)
-    send_queries(1)
     pack_queries(0, qgb, lrb, qp, gp)
     pass_bias(0)
+
+    def block_of(t):
+        return (x + 2 + 3 * t + 3 * (t // 2) + 2 * (t // 3)) % 4
 
     def block(n, carry):
         h = n // 4
         t = n % 4
-        xk = (x + z + 1 + t) % 4
+        xk = block_of(t)
 
         @pl.when(n == 4)
         def _():
@@ -323,25 +372,40 @@
             kvb.at[h, xk], qp.at[h], gp.at[h], bb.at[h, xk], dkv.at[h, xk], dqb.at[h],
             dbb.at[h, xk], scr, t == 0,
         )
-        pl.when(xk != z)(
-            remote(
-                dbb.at[h, xk], rb.at[h, z], dbs.at[h, xk], dbr.at[h, z], place(xk, a, k, x, b)
-            ).start
-        )
-        for dk in (0, 1):
-            d = (k + dk) % 2
-            copy = remote(
-                dkv.at[h, xk, d], rkv.at[h, x, k], dks.at[h, xk, dk], dkr.at[h, x, k],
-                place(z, a, d, xk, b),
-            )
-            if dk == 0:
-                pl.when(xk != x)(copy.start)
-            else:
-                copy.start()
+        send_bias_grad(h, xk)
+
+        @pl.when(n > 0)
+        def _():
+            finish_bias_grad((n - 1) // 4, block_of((n - 1) % 4))
+
+
+        @pl.when(t == 0)
+        def _():
+            for d, dx in ((0, 1), (1, 3)):
+                remote(
+                    dkv.at[h, xk, d], rel.at[h, d], rls.at[h, d], rlr.at[h, d], at(dx=dx)
+                ).start()
+
+        @pl.when(t == 1)
+        def _():
+            send_key_grads(h, right, 1)
+
+        @pl.when(t == 2)
+        def _():
+            add_passed(h, right, 0)
+            send_key_grads(h, right, 0)
+            send_key_grads(h, left, 0)
+
+        @pl.when(t == 3)
+        def _():
+            send_key_grads(h, x, 1 - k)
+            add_passed(h, left, 1)
+            send_key_grads(h, left, 1)
 
         @pl.when(n == 0)
         def _():
             spread_bias(1)
+            send_queries(1)
 
         @pl.when(n == 1)
         def _():
@@ -362,16 +426,14 @@
         return carry
 
     lax.fori_loop(0, 8, block, 0)
+    finish_bias_grad(1, x)
     send_query_grads(1)
-    sum_bias(1)
 
     for h in range(2):
-        for dx in range(4):
-            for dk in range(2):
-                if dx or dk:
-                    xk = (x + dx) % 4
-                    c = (k + dk) % 2
-                    done(rkv.at[h, xk, c], dkr.at[h, xk, c])
+        done(rkv.at[h, x, 1 - k], dkr.at[h, x, 1 - k])
+        for xk in (right, left):
+            for c in range(2):
+                done(rkv.at[h, xk, c], dkr.at[h, xk, c])
 
     def join(own, other):
         low = jnp.where(k == 0, own, other)
@@ -384,12 +446,12 @@
     for j in range(5):
         for which, out in ((0, dk_ref), (1, dv_ref)):
             own = rows(dkv, x, k, which, j)
-            for dx in (1, 2, 3):
-                own = own + rows(rkv, (x + dx) % 4, k, which, j)
-            other = rows(rkv, 0, 1 - k, which, j)
-            for xk in (1, 2, 3):
+            other = rows(rkv, x, 1 - k, which, j)
+            for xk in (right, left):
+                own = own + rows(rkv, xk, k, which, j)
                 other = other + rows(rkv, xk, 1 - k, which, j)
             out[j] = join(own, other)
+    sum_bias(1)
     for h in range(2):
         for dy, dk in ((1, 0), (1, 1), (0, 1)):
             done(rdq.at[h, (b + dy) % 2, (k + dk) % 2], dqr.at[h, (b + dy) % 2, (k + dk) % 2])
@@ -407,10 +469,11 @@
     for h in range(2):
         for i in range(7):
             done(skv.at[0, 0], kvs.at[h, i])
-        for dx in range(4):
-            done(dkv.at[0, 0, 0], dks.at[h, (x + dx) % 4, 1])
-            if dx:
-                done(dkv.at[0, 0, 0], dks.at[h, (x + dx) % 4, 0])
+        done(dkv.at[0, 0, 0], dks.at[h, x, 1 - k])
+        for d in range(2):
+            done(dkv.at[0, 0, 0], dks.at[h, right, d])
+            done(dkv.at[0, 0, 0], dks.at[h, left, d])
+            done(rel.at[0, 0], rls.at[h, d])
         for dy, dk in ((1, 0), (1, 1), (0, 1)):
             done(sqg.at[0, 0], qgs.at[h, dy, dk])
             done(dqb.at[0, 0, 0], dqs.at[h, dy, dk])
@@ -418,8 +481,10 @@
             done(sbb.at[0, 0], d1s.at[h, dy, dk])
         for i in range(6):
             done(bb.at[0, 0, 0], b2s.at[h, i])
-        for dz in (1, 2, 3):
-            done(dbb.at[0, 0], dbs.at[h, (z + dz) % 4])
+        for to in range(2):
+            done(zrel.at[0, 0], zls.at[h, to])
+            for half in range(2):
+                done(zrel.at[0, 0], dbs.at[h, to, half])
     for dy, dk in ((1, 0), (1, 1), (0, 1)):
         done(slr.at[0], lrs.at[dy, dk])
 
@@ -454,15 +519,17 @@
             f(2, 4, 2, 2, 5, 32, 256),
             f(2, 4, 2, 2, 5, 32, 256),
             f(2, 2, 2, 5, 32, 256),
+            f(2, 2, 2, 128, 256),
+            f(2, 2, 2, 5, 32, 256),
             f(2, 2, 2, 5, 32, 256),
             f(2, 4, 2, 2, 128, 256),
-            f(2, 4, 2, 2, 128, 256),
+            f(2, 2, 2, 2, 128, 256),
             f(2, 2, 2, 128, 256),
             pltpu.VMEM((2, 2, 5, 128, 512), BF),
             pltpu.VMEM((2, 2, 5, 128, 512), BF),
             pltpu.VMEM((2, 4, 256, 512), BF),
             dma(2, 7), dma(2, 4, 2), *pair, dma(2, 2), dma(2, 2), *pair, dma(2, 6), dma(2, 4, 2),
-            dma(2, 4, 2), dma(2, 4, 2), *pair, dma(2, 4), dma(2, 4), *pair,
+            dma(2, 4, 2), dma(2, 4, 2), dma(2, 2), dma(2, 2), *pair, dma(2, 2), dma(2, 2), dma(2, 2, 2), dma(2, 2, 2), *pair,
         ],
         compiler_params=pltpu.CompilerParams(
             collective_id=0, has_side_effects=True, vmem_limit_bytes=60 * 2**20

time: 152 us -> 139 us (0.914)
  the two profiles are of different devices: /device:TPU:11 before, /device:TPU:9 now
where the time goes in v3:
time: 139 us
  Pallas kernels  132 us (95%)
  local copies, waits for them, and re-layouts  5.43 us (4%)
    pallas_call x1, Pallas kernels, body(): pl.pallas_call(kernel, out_shape=[jax.ShapeDtypeStruct((5, 256, 128), F32...  132 us
    unnamed x10, local copies, waits for them, and re-layouts  5.43 us

profile of v3, /device:TPU:9, one launch (start us, length us, event | category | flops | bytes accessed | tf_op | source)
XLA Modules:
  0.0 138.5 jit_solution(6375674225241809176)
XLA Ops:
  0.6 132.5 %shard_map.111 = (f32[5,256,128]{2,1,0:T(8,128)}, f32[5,256,128]{2,1,0:T(8,128)}, f32[5,256,128]{2,1,0:T(8,128)}, f32[4,128,256]{2,1,0:T(8,128)}) custom-call(f32[5,256,128]{2,1,0:T(8,128)} %bitcast.13, f32[5,256,128]{2,1,0:T(8,128)} %bitcast.14, f32[5,256,128]{2,1,0:T(8,128)} %bitcast.15, f32[5,256,128]{2,1,0:T(8,128)} %bitcast.16, f32[4,128,256]{2,1,0:T(8,128)} %b_ref.1, ...), custom_call_target="tpu_custom_call" | custom-call | tf_op jit(solution)/shard_map/pallas_call | solution.py:504
  133.1 0.0 copy-start.1
  133.1 2.0 %copy.16 = f32[256,5,128]{2,0,1:T(8,128)} copy(f32[256,5,128]{2,0,1:T(8,128)} %bitcast.12) | data formatting | bytes 1310720
  135.1 0.0 copy-done.1
  135.1 0.0 copy-start
  135.1 0.8 copy.17
  136.0 0.5 copy-done
  136.5 0.0 copy-start.2
  136.5 0.8 copy.18
  137.3 0.4 copy-done.2
  137.7 0.8 copy.19
Async XLA Ops:
  133.1 2.0 %copy-start.1 = (f32[5,256,128]{2,1,0:T(8,128)S(1)}, f32[5,256,128]{2,1,0:T(8,128)}, u32[]{:S(2)}) copy-start(f32[5,256,128]{2,1,0:T(8,128)} %get-tuple-element.9) | copy-start | bytes 1966084
  135.1 1.3 copy-start
  136.5 1.3 copy-start.2

commit v4 on v3

--- a/solution.py
+++ b/solution.py
@@ -77,7 +77,7 @@
         for part in range(2):
             db[half, part] = jnp.zeros((128, 256), F32)
 
-    def step(j, carry):
+    def column(j):
         keys = [None, None]
         scores = [None, None]
         grads = [None, None]
@@ -88,7 +88,7 @@
             scores[src] = dg(kp, qp[src, j], 0, 0)
             grads[src] = dg(vp, gp[src, j], 0, 0)
         for src in range(2):
-            w_hi, w_low, s_hi, s_low = [scr.at[src, i] for i in range(4)]
+            w_hi, w_low, s_hi, s_low = [scr.at[2 * (j % 2) + src, i] for i in range(4)]
             for half in range(2):
                 cols = slice(256 * half, 256 * half + 256)
                 for part in range(2):
@@ -99,7 +99,7 @@
                     w_hi[rows, cols], w_low[rows, cols] = split(w)
                     s_hi[rows, cols], s_low[rows, cols] = split(ds)
         for src in range(2):
-            w_hi, w_low, s_hi, s_low = [scr.at[src, i] for i in range(4)]
+            w_hi, w_low, s_hi, s_low = [scr.at[2 * (j % 2) + src, i] for i in range(4)]
             k_hi, k_low = keys[src]
             r = dg(jnp.concatenate([k_hi, k_low], axis=0), s_hi[...], 1, 0)
             total = (r[:32] + r[32:] + dg(k_hi, s_low[...], 1, 0)) * ROOT
@@ -112,9 +112,9 @@
             r = dg(gp[src, j, 32:96, :], w_hi[...], 1, 1)
             r2 = dg(gp[src, j, 0:32, :], w_low[...], 1, 1)
             dkv[src, 1, j] = r[:32] + r[32:] + r2
-        return carry
-
-    lax.fori_loop(0, 5, step, 0)
+
+    for j in range(5):
+        column(j)
 
 
 def kernel(
@@ -345,13 +345,13 @@
     spread_bias(0)
     pass_keys(0)
     send_keys(1)
+    pass_bias(0)
     for half in range(2):
         for src in range(2):
             done(lrb.at[half, src], lrr.at[half, src])
     wait_queries(0)
     send_bias(1)
     pack_queries(0, qgb, lrb, qp, gp)
-    pass_bias(0)
 
     def block_of(t):
         return (x + 2 + 3 * t + 3 * (t // 2) + 2 * (t // 3)) % 4
@@ -373,11 +373,7 @@
             dbb.at[h, xk], scr, t == 0,
         )
         send_bias_grad(h, xk)
-
-        @pl.when(n > 0)
-        def _():
-            finish_bias_grad((n - 1) // 4, block_of((n - 1) % 4))
-
+        pl.when(t == 3)(lambda: send_query_grads(h))
 
         @pl.when(t == 0)
         def _():
@@ -402,6 +398,10 @@
             add_passed(h, left, 1)
             send_key_grads(h, left, 1)
 
+        @pl.when(n > 0)
+        def _():
+            finish_bias_grad((n - 1) // 4, block_of((n - 1) % 4))
+
         @pl.when(n == 0)
         def _():
             spread_bias(1)
@@ -415,11 +415,7 @@
         def _():
             pass_bias(1)
 
-        @pl.when(n == 3)
-        def _():
-            send_query_grads(0)
-
-        @pl.when(n == 5)
+        @pl.when(n == 6)
         def _():
             sum_bias(0)
 
@@ -427,7 +423,6 @@
 
     lax.fori_loop(0, 8, block, 0)
     finish_bias_grad(1, x)
-    send_query_grads(1)
 
     for h in range(2):
         done(rkv.at[h, x, 1 - k], dkr.at[h, x, 1 - k])
@@ -493,6 +488,11 @@
         for h in range(2):
             done(sbb.at[0, 0], b1s.at[h, 0, 0])
             done(sbb.at[0, 0], d1s.at[h, 0, 0])
+
+
+def hand_over(*refs):
+    for i in range(4):
+        refs[4 + i][...] = refs[i][...]
 
 
 def body(query_proj, key_proj, value_proj, out_grad, pair_bias, log_sum_exp, correction, pad_mask):
@@ -527,7 +527,7 @@
             f(2, 2, 2, 128, 256),
             pltpu.VMEM((2, 2, 5, 128, 512), BF),
             pltpu.VMEM((2, 2, 5, 128, 512), BF),
-            pltpu.VMEM((2, 4, 256, 512), BF),
+            pltpu.VMEM((4, 4, 256, 512), BF),
             dma(2, 7), dma(2, 4, 2), *pair, dma(2, 2), dma(2, 2), *pair, dma(2, 6), dma(2, 4, 2),
             dma(2, 4, 2), dma(2, 4, 2), dma(2, 2), dma(2, 2), *pair, dma(2, 2), dma(2, 2), dma(2, 2, 2), dma(2, 2, 2), *pair,
         ],
@@ -538,7 +538,19 @@
         swap(query_proj), swap(key_proj), swap(value_proj), swap(out_grad), pair_bias,
         swap(log_sum_exp), swap(correction), pad_mask.reshape(16, 128),
     )
-    return swap(dq), swap(dk), swap(dv), db
+    flat = lambda y: y.reshape(1280, 128)
+    rows = pl.BlockSpec((320, 128), lambda i: (i, 0))
+    plane = pl.BlockSpec((1, 128, 256), lambda i: (i, 0, 0))
+    dq, dk, dv, db = pl.pallas_call(
+        hand_over,
+        grid=(4,),
+        out_shape=[jax.ShapeDtypeStruct((1280, 128), F32)] * 3
+        + [jax.ShapeDtypeStruct((4, 128, 256), F32)],
+        in_specs=[rows] * 3 + [plane],
+        out_specs=[rows] * 3 + [plane],
+    )(flat(dq), flat(dk), flat(dv), db)
+    whole = lambda y: swap(y.reshape(5, 256, 128))
+    return whole(dq), whole(dk), whole(dv), db
 
 
 def solution(mesh):

time: 139 us -> 135 us (0.971)
  local copies, waits for them, and re-layouts: 5.43 us -> 0 us
  Pallas kernels: 132 us -> 134 us
    unnamed x10 -> x0, local copies, waits for them, and re-layouts: 5.43 us -> none
    pallas_call x0 -> x1, Pallas kernels: none -> 3.97 us  [body(): pl.pallas_call(hand_over, grid=(4,), out_shape=[jax.ShapeDtypeStruct((128...]
    pallas_call x1, Pallas kernels: 132 us -> 130 us  [body(): pl.pallas_call(kernel, out_shape=[jax.ShapeDtypeStruct((5, 256, 128), F32...]
where the time goes in v4:
time: 135 us; the launch traced here: 134 us
  Pallas kernels  134 us (99%)
    pallas_call x1, Pallas kernels, body(): pl.pallas_call(kernel, out_shape=[jax.ShapeDtypeStruct((5, 256, 128), F32...  130 us
    pallas_call x1, Pallas kernels, body(): pl.pallas_call(hand_over, grid=(4,), out_shape=[jax.ShapeDtypeStruct((128...  3.97 us

profile of v4, /device:TPU:9, one launch (start us, length us, event | category | flops | bytes accessed | tf_op | source)
XLA Modules:
  0.0 134.3 jit_solution(2542221204499506158)
XLA Ops:
  0.6 129.7 %shard_map.111 = (f32[5,256,128]{2,1,0:T(8,128)}, f32[5,256,128]{2,1,0:T(8,128)}, f32[5,256,128]{2,1,0:T(8,128)}, f32[4,128,256]{2,1,0:T(8,128)}) custom-call(f32[5,256,128]{2,1,0:T(8,128)} %bitcast.19, f32[5,256,128]{2,1,0:T(8,128)} %bitcast.20, f32[5,256,128]{2,1,0:T(8,128)} %bitcast.21, f32[5,256,128]{2,1,0:T(8,128)} %bitcast.22, f32[4,128,256]{2,1,0:T(8,128)} %b_ref.1, ...), custom_call_target="tpu_custom_call" | custom-call | tf_op jit(solution)/shard_map/pallas_call | solution.py:504
  130.4 4.0 %shard_map.112 = (f32[1280,128]{1,0:T(8,128)}, f32[1280,128]{1,0:T(8,128)}, f32[1280,128]{1,0:T(8,128)}, f32[4,128,256]{2,1,0:T(8,128)}) custom-call(f32[1280,128]{1,0:T(8,128)} %bitcast.23, f32[1280,128]{1,0:T(8,128)} %bitcast.24, f32[1280,128]{1,0:T(8,128)} %bitcast.25, f32[4,128,256]{2,1,0:T(8,128)} %get-tuple-element.15.refs_3_), custom_call_target="tpu_custom_call" | custom-call | tf_op jit(solution)/shard_map/pallas_call | solution.py:544

commit v5 on v4

--- a/solution.py
+++ b/solution.py
@@ -50,23 +50,23 @@
     return hi, low, jnp.concatenate([hi, low, hi, ones], axis=0)
 
 
-def pack_queries(h, qgb, lrb, qp, gp):
+def pack_queries(h, half, qgb, lrb, qp, gp):
+    cols = pl.ds(pl.multiple_of(256 * half, 256), 256)
+
     def step(j, carry):
         for src in range(2):
-            for half in range(2):
-                cols = slice(256 * half, 256 * half + 256)
-                level = lrb[half, src, 0, h, pl.ds(j, 1), :] * (-LOG2E)
-                corr = -lrb[half, src, 1, h, pl.ds(j, 1), :]
-                for which, packed, scale, row in (
-                    (0, qp, LOG2E * ROOT, level),
-                    (1, gp, None, corr),
-                ):
-                    x = qgb[h, half, src, which, j]
-                    hi, low = split(x if scale is None else x * scale)
-                    packed[h, src, j, 0:32, cols] = hi
-                    packed[h, src, j, 32:64, cols] = hi
-                    packed[h, src, j, 64:96, cols] = low
-                    packed[h, src, j, 96:128, cols] = extra_rows(row)
+            level = lrb[half, src, 0, h, pl.ds(j, 1), :] * (-LOG2E)
+            corr = -lrb[half, src, 1, h, pl.ds(j, 1), :]
+            for which, packed, scale, row in (
+                (0, qp, LOG2E * ROOT, level),
+                (1, gp, None, corr),
+            ):
+                x = qgb[h, half, src, which, j]
+                hi, low = split(x if scale is None else x * scale)
+                packed[h, src, j, 0:32, cols] = hi
+                packed[h, src, j, 32:64, cols] = hi
+                packed[h, src, j, 64:96, cols] = low
+                packed[h, src, j, 96:128, cols] = extra_rows(row)
         return carry
 
     lax.fori_loop(0, 5, step, 0)
@@ -231,19 +231,29 @@
         pl.when(xk != left)(lambda: done(kvb.at[h, xk, 0], kvr.at[h, xk, 0]))
         pl.when(xk != right)(lambda: done(kvb.at[h, xk, 1], kvr.at[h, xk, 1]))
 
+    def share_queries(h):
+        pltpu.make_async_copy(sqg.at[h, k], qgb.at[h, b, k], qgr.at[h, b, k]).start()
+        push_queries(h, ((0, 1),))
+
     def send_queries(h):
-        pltpu.make_async_copy(sqg.at[h, k], qgb.at[h, b, k], qgr.at[h, b, k]).start()
-        for dy, dk in ((1, 0), (1, 1), (0, 1)):
+        push_queries(h, ((1, 0), (1, 1)))
+
+    def push_queries(h, steps):
+        for dy, dk in steps:
             d = (k + dk) % 2
             remote(
                 sqg.at[h, d], qgb.at[h, b, k], qgs.at[h, dy, dk], qgr.at[h, b, k],
                 place(z, a, d, x, (b + dy) % 2),
             ).start()
 
-    def wait_queries(h):
-        for half in range(2):
-            for src in range(2):
-                done(qgb.at[h, half, src], qgr.at[h, half, src])
+    def take_queries(h, half):
+        for src in range(2):
+            done(qgb.at[h, half, src], qgr.at[h, half, src])
+        pack_queries(h, half, qgb, lrb, qp, gp)
+
+    def wait_levels(half):
+        for src in range(2):
+            done(lrb.at[half, src], lrr.at[half, src])
 
     def push_bias_grad(h, to, half):
         zk = (up, down)[to]
@@ -341,17 +351,19 @@
         ).start()
     turn(q_ref, sqg, 0)
     turn(g_ref, sqg, 1)
+    share_queries(0)
     send_queries(0)
+    share_queries(1)
     spread_bias(0)
     pass_keys(0)
     send_keys(1)
     pass_bias(0)
-    for half in range(2):
-        for src in range(2):
-            done(lrb.at[half, src], lrr.at[half, src])
-    wait_queries(0)
+    wait_levels(b)
+    take_queries(0, b)
+    take_queries(1, b)
+    wait_levels(1 - b)
+    take_queries(0, 1 - b)
     send_bias(1)
-    pack_queries(0, qgb, lrb, qp, gp)
 
     def block_of(t):
         return (x + 2 + 3 * t + 3 * (t // 2) + 2 * (t // 3)) % 4
@@ -363,8 +375,7 @@
 
         @pl.when(n == 4)
         def _():
-            wait_queries(1)
-            pack_queries(1, qgb, lrb, qp, gp)
+            take_queries(1, 1 - b)
 
         wait_keys(h, xk)
         wait_bias(h, xk)

time: 135 us -> 135 us (level)
  no operation moved by 1% of the time
where the time goes in v5:
time: 135 us; the launch traced here: 134 us
  Pallas kernels  134 us (99%)
    pallas_call x1, Pallas kernels, body(): pl.pallas_call(kernel, out_shape=[jax.ShapeDtypeStruct((5, 256, 128), F32...  130 us
    pallas_call x1, Pallas kernels, body(): pl.pallas_call(hand_over, grid=(4,), out_shape=[jax.ShapeDtypeStruct((128...  3.97 us

profile of v5, /device:TPU:9, one launch (start us, length us, event | category | flops | bytes accessed | tf_op | source)
XLA Modules:
  0.0 134.4 jit_solution(14200861918769806483)
XLA Ops:
  0.6 129.8 %shard_map.111 = (f32[5,256,128]{2,1,0:T(8,128)}, f32[5,256,128]{2,1,0:T(8,128)}, f32[5,256,128]{2,1,0:T(8,128)}, f32[4,128,256]{2,1,0:T(8,128)}) custom-call(f32[5,256,128]{2,1,0:T(8,128)} %bitcast.19, f32[5,256,128]{2,1,0:T(8,128)} %bitcast.20, f32[5,256,128]{2,1,0:T(8,128)} %bitcast.21, f32[5,256,128]{2,1,0:T(8,128)} %bitcast.22, f32[4,128,256]{2,1,0:T(8,128)} %b_ref.1, ...), custom_call_target="tpu_custom_call" | custom-call | tf_op jit(solution)/shard_map/pallas_call | solution.py:515
  130.5 4.0 %shard_map.112 = (f32[1280,128]{1,0:T(8,128)}, f32[1280,128]{1,0:T(8,128)}, f32[1280,128]{1,0:T(8,128)}, f32[4,128,256]{2,1,0:T(8,128)}) custom-call(f32[1280,128]{1,0:T(8,128)} %bitcast.23, f32[1280,128]{1,0:T(8,128)} %bitcast.24, f32[1280,128]{1,0:T(8,128)} %bitcast.25, f32[4,128,256]{2,1,0:T(8,128)} %get-tuple-element.15.refs_3_), custom_call_target="tpu_custom_call" | custom-call | tf_op jit(solution)/shard_map/pallas_call | solution.py:555
